TPU v7x, 512 devices: a whole 4x8x8 slice. The times are simulated.
512 devices in a mesh: visit: 8 (over x, core), patch: 64 (over y, z).
Axes of the slice: x: 4, y: 8, z: 8, core: 2. Of those that a mesh axis runs over, the one named last changes fastest.
Arguments:
- template: bfloat16 [64, 8, 16, 2304], P('patch', 'visit'), may hold values from -5 to 5
- science: bfloat16 [8, 64, 8, 16, 1024], P('visit', 'patch'), may hold values from -12 to 12
- weight: bfloat16 [8, 64, 8, 16], P('visit', 'patch'), may hold values from 0.5 to 2
- stamp_patch: int32 [64, 8, 16], P('patch', 'visit'), may hold values from 0 to 63, as said below
- basis_across: float32 [43, 17], replicated, may hold values from -0.6 to 0.6
- basis_down: float32 [43, 17], replicated, may hold values from -0.6 to 0.6
Outputs:
- kernel_coef: float32 [8, 64, 43], P('visit', 'patch')
- residual: float32 [8, 64, 8, 16], P(None, 'patch', 'visit')
Inputs may be any that keep to these rules, and one draw needn't show every extreme that they name: `stamp_patch`: the stamps of detector d lie in patches d - 1, d, d + 1, d + 2 (modulo 64), patch d always among them; in every draw some detector has stamps in its patch d - 1. Every one of the 64 patches holds at least one stamp.
All inputs are finite; a program needn't handle non-finite values.
Results may differ from a plain program's by a relative error of at most 0.0057.
Values may be sent and summed in bfloat16 or wider, within the bound.
A program may use at most 128 MiB of HBM per device.

v0:
```python
import jax
import jax.numpy as jnp
from jax import lax
from jax.sharding import PartitionSpec as P

STAMP = 32


highest = lax.Precision.HIGHEST


def conv_tables(basis_across, basis_down, stamp_size):
    basis_count, taps = basis_across.shape
    template_size = stamp_size + taps - 1
    offset = jnp.arange(template_size)[:, None] - jnp.arange(stamp_size)[None, :]
    select = (offset[None, :, :] == jnp.arange(taps)[:, None, None]).astype(jnp.float32)
    across = basis_across.astype(jnp.bfloat16).astype(jnp.float32)
    downward = basis_down.astype(jnp.bfloat16).astype(jnp.float32)
    row_table = jnp.einsum("kj,jzx->zkx", across, select, precision=highest)
    row_table = row_table.reshape(template_size, basis_count * stamp_size).astype(jnp.bfloat16)
    col_table = jnp.einsum("kj,jzy->kyz", downward, select, precision=highest).astype(jnp.bfloat16)
    return (row_table, col_table)


def basis_images(stamps, row_table, col_table, stamp_size):
    stamp_count = stamps.shape[0]
    template_size = row_table.shape[0]
    basis_count = col_table.shape[0]
    across = jnp.dot(
        stamps.reshape(stamp_count * template_size, template_size),
        row_table,
        preferred_element_type=jnp.float32,
    )
    across = across.astype(jnp.bfloat16).reshape(
        stamp_count, template_size, basis_count, stamp_size
    )
    images = jnp.einsum("kyz,szkx->skyx", col_table, across, preferred_element_type=jnp.float32)
    return images.astype(jnp.bfloat16).reshape(stamp_count, basis_count, stamp_size * stamp_size)


def padded(total):
    return (total + 127) // 128 * 128


def solve_systems(matrices, rhs):
    factor = jnp.linalg.cholesky(matrices)
    inner = jax.scipy.linalg.solve_triangular(factor, rhs[..., None], lower=True)
    return jax.scipy.linalg.solve_triangular(factor, inner, lower=True, trans=1)[..., 0]


def solve_packed(packed_rows, basis_count):
    square = basis_count * basis_count
    matrices = packed_rows[:, :square].reshape(-1, basis_count, basis_count)
    rhs = packed_rows[:, square : square + basis_count]
    return solve_systems(matrices, rhs)


def on_device(template, science, weight, stamp_patch, basis_across, basis_down):
    basis_count = basis_across.shape[0]
    received, recv_weight = (
        lax.all_to_all(science, "visit", split_axis=2, concat_axis=0, tiled=True),
        lax.all_to_all(weight, "visit", split_axis=2, concat_axis=0, tiled=True),
    )
    visit_count = received.shape[0]
    stamp_count = template.shape[2]
    pixels = received.shape[-1]
    exposures = received.reshape(visit_count, stamp_count, pixels)
    weights = recv_weight.reshape(visit_count, stamp_count).astype(jnp.float32)
    stamps = template.reshape(stamp_count, template.shape[3])
    owners = stamp_patch.reshape(stamp_count)
    patch_count = lax.axis_size("patch")
    system_count = visit_count * patch_count
    row_table, col_table = conv_tables(basis_across, basis_down, STAMP)
    block_count = stamp_count // stamp_count

    def first_pass(block_index):
        images = basis_images(stamps, row_table, col_table, STAMP)
        gram_rows = jnp.einsum("skp,sjp->skj", images, images, preferred_element_type=jnp.float32)
        project_rows = jnp.einsum(
            "vsp,skp->vsk", exposures, images, preferred_element_type=jnp.float32
        )
        return (gram_rows, project_rows)

    gram_blocks, project_blocks = lax.map(first_pass, jnp.arange(block_count))
    gram = gram_blocks.reshape(stamp_count, basis_count * basis_count)
    project = jnp.transpose(project_blocks, (1, 0, 2, 3)).reshape(
        visit_count, stamp_count, basis_count
    )
    packed_width = padded(gram.shape[1] + basis_count)
    member = (owners[:, None] == jnp.arange(patch_count)[None, :]).astype(jnp.float32)
    weighted = weights.T[:, :, None] * member[:, None, :]
    rhs = jnp.einsum("svq,vsk->vqk", weighted, project, precision=highest)
    flat_weights = weighted.reshape(stamp_count, system_count)
    flat_rhs = rhs.reshape(system_count, basis_count)
    matrix_rows = jnp.dot(
        flat_weights.T, gram, precision=highest, preferred_element_type=jnp.float32
    )
    joined = jnp.concatenate([matrix_rows, flat_rhs], axis=-1)
    widths = [(0, 0)] * (joined.ndim - 1) + [(0, packed_width - joined.shape[-1])]
    mine = lax.psum_scatter(
        jnp.pad(joined, widths), ("visit", "patch"), scatter_dimension=0, tiled=True
    )
    own = solve_packed(mine, basis_count)
    coefs = lax.all_gather(own, ("visit", "patch"), axis=0, tiled=True)
    stamp_coef = jnp.einsum(
        "sq,vqk->vsk",
        member,
        coefs.reshape(visit_count, patch_count, basis_count),
        precision=highest,
    ).astype(jnp.bfloat16)

    def second_pass(block_index):
        images = basis_images(stamps, row_table, col_table, STAMP)
        model = jnp.einsum("vsk,skp->vsp", stamp_coef, images, preferred_element_type=jnp.float32)
        diff = exposures.astype(jnp.float32) - model
        return weights * jnp.mean(diff * diff, axis=2)

    blocks = lax.map(second_pass, jnp.arange(block_count))
    residual = jnp.transpose(blocks, (1, 0, 2)).reshape(visit_count, 1, 1, stamp_count)
    kernel_coef = own.reshape(1, 1, basis_count)
    return (kernel_coef, residual)


def solution(mesh):
    return jax.shard_map(
        on_device,
        mesh=mesh,
        in_specs=(
            P("patch", "visit", None, None),
            P("visit", "patch", None, None, None),
            P("visit", "patch", None, None),
            P("patch", "visit", None),
            P(),
            P(),
        ),
        out_specs=(P("visit", "patch", None), P(None, "patch", "visit", None)),
        check_vma=False,
    )
```

profile of v0, /device:TPU:1, one launch (start us, length us, event | category | flops | bytes accessed | tf_op | source)
XLA Modules:
  0.0 636.2 jit_solution(16936831435310888613)
XLA Ops:
  7.2 1.3 copy.46
  8.4 10.1 %all-to-all-start = ((bf16[1,1,8,16]{3,1,0,2:T(2,128)(2,1)}), bf16[1,1,8,16]{3,1,0,2:T(2,128)(2,1)S(1)}, u32[]{:S(2)}, u32[]{:S(2)}) async-start(bf16[1,1,8,16]{3,1,0,2:T(2,128)(2,1)} %copy.46), calls=%async_computation | async-start | bytes 8192 | tf_op jit(solution)/shard_map/all_to_all | solution.py:62
  18.5 1.1 fusion.7
  19.7 0.7 copy.49
  20.3 1.1 reshape_reshape.6
  21.5 2.1 fusion.4
  23.5 9.2 %reshape.178 = bf16[16,48,43,32]{1,0,3,2:T(8,128)(2,1)} reshape(bf16[768,1376]{0,1:T(8,128)(2,1)} %fusion.4) | data formatting | bytes 4227072 | tf_op jit(solution)/shard_map/while/body/eval_jaxpr/reshape | solution.py:34
  32.7 0.4 fusion.8
  33.2 0.7 copy.67
  33.8 6.7 %convert_bitcast_fusion = bf16[16,43,32,32]{2,3,0,1:T(8,128)(2,1)} fusion(bf16[43,32,48,1]{2,1,3,0:T(8,128)(2,1)S(1)} %copy.67, bf16[16,48,43,32]{1,0,3,2:T(8,128)(2,1)} %reshape.178), kind=kOutput, calls=%fused_computation.2 | convolution fusion | flops 68337664 | bytes 3654656 | tf_op jit(solution)/shard_map/while/body/eval_jaxpr/kyz,szkx->skyx/dot_general | solution.py:37
  40.6 8.3 %copy.73 = bf16[16,43,32,32]{3,2,1,0:T(8,128)(2,1)} copy(bf16[16,43,32,32]{2,3,0,1:T(8,128)(2,1)} %convert_bitcast_fusion) | data formatting | bytes 2818048 | tf_op jit(solution)/shard_map/while/body/eval_jaxpr/reshape | solution.py:38
  48.8 7.6 %reshape.203 = bf16[16,43,1024]{2,1,0:T(8,128)(2,1)S(1)} reshape(bf16[16,43,32,32]{3,2,1,0:T(8,128)(2,1)} %copy.73) | data formatting | bytes 2818048 | tf_op jit(solution)/shard_map/while/body/eval_jaxpr/reshape | solution.py:38
  56.4 0.5 fusion.33
  57.2 4.8 all-to-all-start.1
  62.3 5.0 fusion.34
  67.4 1.2 all-to-all-done.1
  68.6 0.5 convolution_bitcast_fusion.1
  69.1 0.5 fusion.15
  69.8 4.4 select_maximum_fusion
  74.3 282.5 %all-reduce.8.cloned.1.call-done = f32[512,1920]{0,1:T(8,128)} async-done(((f32[512,1920]{0,1:T(8,128)}), f32[512,1920]{0,1:T(8,128)}) %all-reduce.8.cloned.1.call-update) | async-done | bytes 3932176
  356.8 1.8 dynamic-slice_reduce_fusion
  358.8 3.9 custom-call.11
  362.8 0.6 compare_reduce_fusion
  363.4 0.7 select_select_fusion
  364.1 3.3 custom-call.12
  367.4 0.9 dynamic-slice_reduce_fusion.1
  368.8 0.6 copy-done
  369.4 257.5 %all-reduce.6.cloned.1.call-done = f32[22016]{0:T(1024)} async-done(((f32[22016]{0:T(1024)}), f32[22016]{0:T(1024)}) %all-reduce.6.cloned.1.call-update) | async-done | bytes 88080
  626.9 1.1 reshape.185
  628.1 0.2 fusion.10
  628.3 0.4 fusion.9
  628.8 0.6 fusion.30
  (30 shorter events, 1.5 us)
Async XLA Ops:
  8.4 48.8 %all-to-all-start = ((bf16[1,1,8,16]{3,1,0,2:T(2,128)(2,1)}), bf16[1,1,8,16]{3,1,0,2:T(2,128)(2,1)S(1)}, u32[]{:S(2)}, u32[]{:S(2)}) async-start(bf16[1,1,8,16]{3,1,0,2:T(2,128)(2,1)} %copy.46), calls=%async_computation | async-start | bytes 8192 | tf_op jit(solution)/shard_map/all_to_all | solution.py:62
  23.5 9.2 %copy-start.1 = (f32[43,17]{0,1:T(8,128)S(1)}, f32[43,17]{0,1:T(8,128)}, u32[]{:S(2)}) copy-start(f32[43,17]{0,1:T(8,128)} %param.11) | copy-start | bytes 8776
  48.8 8.1 %copy-start.2 = (s32[1,1,16]{2,1,0:T(1,128)S(1)}, s32[1,1,16]{2,1,0:T(1,128)}, u32[]{:S(2)}) copy-start(s32[1,1,16]{2,1,0:T(1,128)} %param.9) | copy-start | bytes 196
  57.2 11.3 %all-to-all-start.1 = ((bf16[1,1,8,16,1024]{4,3,1,0,2:T(8,128)(2,1)}), bf16[1,1,8,16,1024]{4,3,1,0,2:T(8,128)(2,1)S(1)}, u32[]{:S(2)}, u32[]{:S(2)}) async-start(bf16[1,1,8,16,1024]{4,3,1,0,2:T(8,128)(2,1)} %bitcast.11), calls=%async_computation.1 | async-start | bytes 524288 | tf_op jit(solution)/shard_map/all_to_all | solution.py:61
  62.1 294.8 %all-reduce.8.cloned.1.call-start = ((), (), s32[]{:S(2)}) async-start(), calls=%async_computation.3 | async-start | bytes 7864320
  74.2 552.7 %all-reduce.6.cloned.1.call-start = ((), (), s32[]{:S(2)}) async-start(), calls=%async_computation.2 | async-start | bytes 180224
  368.6 260.8 %copy-start.3 = (f32[1,43]{1,0:T(1,128)}, f32[1,43]{1,0:T(1,128)S(1)}, u32[]{:S(2)}) copy-start(f32[1,43]{1,0:T(1,128)S(1)} %fusion.19) | copy-start | bytes 520
  368.8 0.6 copy-start
Sparse Core Ops, SparseCore 0:
  74.3 282.4 all-reduce.7
  369.6 257.3 all-reduce.5
where the time goes:
time: 637 us; the launch traced here: 636 us
  waiting for transfers between devices  541 us (85%)
  local copies, waits for them, and re-layouts  34.2 us (5%)
  matrix products  17.9 us (3%)
  starting transfers between devices  15 us (2%)
  between operations  14.2 us (2%)
  other arithmetic  13.7 us (2%)
    unnamed x4, waiting for transfers between devices  540 us
    reshape x2, local copies, waits for them, and re-layouts, basis_images(): images.astype(jnp.bfloat16)  15.8 us
  transfers between devices with their start and end apart: 4, of which 3 were waited for; matrix products, arithmetic and copies ran while one was open for 7% of the time, Pallas kernels for 0%

commit v1 on v0

v1 whole, which is shorter than its diff:
```python
import functools

import jax
import jax.numpy as jnp
from jax import lax
from jax.experimental import pallas as pl
from jax.experimental.pallas import tpu as pltpu
from jax.sharding import PartitionSpec as P

MESH = pl.DeviceIdType.MESH
F32 = jnp.float32
BF16 = jnp.bfloat16

STAMP = 32
TAPS = 17
SIDE = 48
NB = 43
REACH = 4


def lanes(shape):
    return lax.broadcasted_iota(jnp.int32, shape, len(shape) - 1)


def tables(basis_across, basis_down):
    across = jnp.pad(basis_across.astype(BF16), ((0, 1), (0, 0)))
    down = jnp.pad(basis_down.astype(BF16), ((0, 5), (0, 0)))
    place = jnp.arange(SIDE)[:, None] - jnp.arange(128)[None, :] % STAMP
    row_table = jnp.zeros((SIDE, 44, 128), BF16)
    for tap in range(TAPS):
        row_table = jnp.where(
            (place == tap)[:, None, :], across[None, :, tap, None], row_table
        )
    place = jnp.arange(256)[None, :] % 32 - jnp.arange(16)[:, None]
    same = jnp.arange(8)[:, None] == jnp.arange(256)[None, :] // 32
    grouped = down.reshape(6, 8, TAPS)
    col_table = jnp.zeros((6, 16, 8, 256), BF16)
    for tap in range(TAPS):
        here = (place == tap)[None, :, None, :] & same[None, None, :, :]
        col_table = jnp.where(here, grouped[:, None, :, tap, None], col_table)
    return row_table.reshape(SIDE, 44 * 128), col_table.reshape(6 * 128, 256)


def inverse_4x4(m):
    p, q, s = m[0][0], m[0][1], m[1][1]
    i = 1.0 / (p * s - q * q)
    a, b, c = s * i, -q * i, p * i
    e, f, g, h = m[0][2], m[0][3], m[1][2], m[1][3]
    ae, af = a * e + b * g, a * f + b * h
    ce, cf = b * e + c * g, b * f + c * h
    t = m[2][2] - (e * ae + g * ce)
    u = m[2][3] - (e * af + g * cf)
    w = m[3][3] - (f * af + h * cf)
    j = 1.0 / (t * w - u * u)
    x, y, z = w * j, -u * j, t * j
    r00, r01 = -(ae * x + af * y), -(ae * y + af * z)
    r10, r11 = -(ce * x + cf * y), -(ce * y + cf * z)
    n00 = a - (r00 * ae + r01 * af)
    n01 = b - (r00 * ce + r01 * cf)
    n11 = c - (r10 * ce + r11 * cf)
    return (
        (n00, n01, r00, r01),
        (n01, n11, r10, r11),
        (r00, r10, x, y),
        (r01, r11, y, z),
    )


def solve(tiles):
    lane = lanes((8, 128))
    tiles = list(tiles)
    for block in range(11):
        first = 4 * block
        tile = tiles[first // 8]
        rows = [
            jnp.broadcast_to(tile[(first + c) % 8 : (first + c) % 8 + 1, :], (8, 128))
            for c in range(4)
        ]
        pivot = [[None] * 4 for _ in range(4)]
        for r in range(4):
            for c in range(r, 4):
                value = jnp.broadcast_to(rows[r][:, first + c : first + c + 1], (8, 128))
                pivot[r][c] = pivot[c][r] = value
        inverse = inverse_4x4(pivot)
        inside = (lane >= first) & (lane < first + 4)
        rows = [
            jnp.where(inside, jnp.where(lane == first + c, -1.0, 0.0), rows[c])
            for c in range(4)
        ]
        scaled = [
            (inverse[r][0] * rows[0] + inverse[r][1] * rows[1])
            + (inverse[r][2] * rows[2] + inverse[r][3] * rows[3])
            for r in range(4)
        ]
        for t in range((first + 4) // 8, 6):
            old = tiles[t]
            cols = [
                jnp.broadcast_to(old[:, first + c : first + c + 1], (8, 128))
                for c in range(4)
            ]
            change = (cols[0] * scaled[0] + cols[1] * scaled[1]) + (
                cols[2] * scaled[2] + cols[3] * scaled[3]
            )
            tiles[t] = jnp.where(inside, 0.0, old) - change
    return tiles[5][7:8, :]


def unpack(low, high):
    lane = lanes((8, 128))
    row = lax.broadcasted_iota(jnp.int32, (8, 128), 0)
    tiles = [low, high]
    tiles += [pltpu.roll(x, 96, 1) for x in (low, high)]
    tiles += [pltpu.roll(x, 80, 1) for x in (low, high)]
    full = jnp.concatenate(tiles, axis=0)
    keep = lanes((SIDE, 128)) // 16 >= lax.broadcasted_iota(jnp.int32, (SIDE, 128), 0) // 16
    upper = jnp.where(keep & (lanes((SIDE, 128)) < SIDE), full, 0.0)
    square = jnp.concatenate([upper, jnp.zeros((128 - SIDE, 128), F32)], axis=0)
    flipped = square.T[:SIDE]
    full = jnp.where(keep, upper, flipped)
    tiles = [full[8 * t : 8 * t + 8] for t in range(6)]
    right = jnp.where(
        lane < 32,
        jnp.broadcast_to(pltpu.roll(low, 32, 1)[0:1], (8, 128)),
        jnp.broadcast_to(pltpu.roll(low, 64, 1)[1:2], (8, 128)),
    )
    right = jnp.where(lane < NB, right, 0.0)
    tiles[5] = jnp.where(row == 7, right, tiles[5])
    tiles[5] = jnp.where((row == 3) & (lane == NB), 1.0, tiles[5])
    return tiles


def kernel(
    visits,
    patches,
    stamps_ref,
    row_ref,
    col_ref,
    weight_ref,
    offset_ref,
    offset_smem,
    science_ref,
    coef_ref,
    residual_ref,
    rows_scr,
    wide_scr,
    image_scr,
    sci_recv,
    sci_scr,
    w_recv,
    gram_scr,
    proj_scr,
    msg,
    inbox,
    coef_row,
    coef_box,
    own_sem,
    sci_send,
    sci_sem,
    w_send,
    w_sem,
    msg_send,
    msg_sem,
    coef_send,
    coef_sem,
):
    me_v = lax.axis_index("visit")
    me_q = lax.axis_index("patch")
    barrier = pltpu.get_barrier_semaphore()
    span = 2 * REACH - 3

    def peer(step):
        v = lax.rem(me_v + lax.rem(step, visits), visits)
        q = lax.rem(me_q + lax.div(step, visits) - 2 + patches, patches)
        return v, q

    @pl.loop(0, span * visits)
    def greet(step):
        @pl.when(step != 2 * visits)
        def _():
            v, q = peer(step)
            pl.semaphore_signal(barrier, inc=1, device_id=(v, q), device_id_type=MESH)

    own_copy = pltpu.make_async_copy(science_ref.at[me_v], sci_recv.at[me_v], own_sem)
    own_copy.start()
    w_recv[pl.ds(me_v, 1), :] = weight_ref[pl.ds(me_v, 1), :]

    pl.semaphore_wait(barrier, span * visits - 1)

    @pl.loop(1, visits)
    def send_science(step):
        v = lax.rem(me_v + step, visits)
        pltpu.make_async_remote_copy(
            src_ref=weight_ref.at[pl.ds(v, 1), :],
            dst_ref=w_recv.at[pl.ds(me_v, 1), :],
            send_sem=w_send,
            recv_sem=w_sem,
            device_id=(v, me_q),
            device_id_type=MESH,
        ).start()
        pltpu.make_async_remote_copy(
            src_ref=science_ref.at[v],
            dst_ref=sci_recv.at[me_v],
            send_sem=sci_send,
            recv_sem=sci_sem,
            device_id=(v, me_q),
            device_id_type=MESH,
        ).start()

    quarter = lax.broadcasted_iota(jnp.int32, (SIDE, 256), 1) % 128 // STAMP
    masks = [(quarter == s).astype(F32).astype(BF16) for s in range(4)]
    stamps = stamps_ref[...]
    rows_scr[44:48] = jnp.zeros((4, SIDE, 512), BF16)

    @pl.loop(0, 22)
    def make_rows(pair):
        table = row_ref[:, pl.ds(pl.multiple_of(pair * 256, 256), 256)]
        right = jnp.concatenate([table * m for m in masks], axis=0)
        out = jnp.dot(stamps, right, preferred_element_type=F32).astype(BF16)
        for j in range(2):
            for g in range(4):
                rows_scr[2 * pair + j, :, 128 * g : 128 * g + 128] = out[
                    SIDE * g : SIDE * g + SIDE, 128 * j : 128 * j + 128
                ]

    @pl.loop(0, 6)
    def make_images(group):
        first = pl.multiple_of(group * 8, 8)
        left = col_ref[pl.ds(pl.multiple_of(group * 128, 128), 128), :]
        for half in range(2):
            right = rows_scr[pl.ds(first, 8), 16 * half : 16 * half + 32, :]
            out = jnp.dot(left, right.reshape(256, 512), preferred_element_type=F32)
            wide_scr[16 * half : 16 * half + 16, pl.ds(first, 8), :] = out.reshape(16, 8, 512)

    lane = lanes((SIDE, 128))
    even = lane // STAMP % 2 == 0
    lower = lane < 64

    @pl.loop(0, 8)
    def regroup(quad):
        for g in range(4):
            part = [
                wide_scr[4 * quad + r, :, 128 * g : 128 * g + 128] for r in range(4)
            ]
            for a, b in ((0, 1), (2, 3)):
                x, y = part[a], part[b]
                part[a] = jnp.where(even, x, pltpu.roll(y, 32, 1))
                part[b] = jnp.where(even, pltpu.roll(x, 96, 1), y)
            for a, b in ((0, 2), (1, 3)):
                x, y = part[a], part[b]
                part[a] = jnp.where(lower, x, pltpu.roll(y, 64, 1))
                part[b] = jnp.where(lower, pltpu.roll(x, 64, 1), y)
            for s in range(4):
                image_scr[4 * g + s, :, pl.ds(pl.multiple_of(quad * 128, 128), 128)] = part[
                    s
                ].astype(BF16)

    own_copy.wait()
    pltpu.make_async_copy(sci_recv.at[1:], sci_recv.at[1:], sci_sem).wait()
    pltpu.make_async_copy(w_recv.at[1:], w_recv.at[1:], w_sem).wait()

    for v in range(8):
        for t in range(8):
            sci_scr[128 * t + 16 * v : 128 * t + 16 * v + 16, :] = sci_recv[
                v, :, 128 * t : 128 * t + 128
            ].astype(F32)

    def exposures(s):
        return [sci_scr[pl.ds(128 * t + s, 8, stride=16), :] for t in range(8)]

    nothing = jnp.zeros((8, 1024), F32)
    lane16 = lanes((16, 128))

    @pl.loop(0, 16)
    def make_grams(s):
        image = image_scr[s]
        science = jnp.concatenate(exposures(s), axis=1)
        left = jnp.concatenate(
            [image, jnp.concatenate([science, nothing], axis=0).astype(BF16)], axis=0
        )
        out = lax.dot_general(
            left, image, (((1,), (1,)), ((), ())), preferred_element_type=F32
        )
        out = jnp.concatenate([out, jnp.zeros((64, 80), F32)], axis=1)
        packed = jnp.where(
            lane16 < 48,
            out[0:16],
            jnp.where(
                lane16 < 80,
                pltpu.roll(out[16:32], 32, 1),
                pltpu.roll(out[32:48], 48, 1),
            ),
        )
        gram_scr[pl.ds(pl.multiple_of(s * 16, 16), 16), :] = packed
        proj_scr[pl.ds(pl.multiple_of(s * 8, 8), 8), :] = out[48:56]

    weights = w_recv[...]
    offset = jnp.broadcast_to(offset_ref[...], (8, 128))
    weighted = jnp.concatenate(
        [jnp.where(offset == o, weights, 0.0) for o in range(REACH)], axis=0
    )
    left = weighted[:, :16].astype(BF16)
    left = jnp.concatenate([left] * 3, axis=1)
    right = jnp.concatenate(
        [gram_scr[pl.ds(r, 16, stride=16), :] for r in range(16)], axis=1
    )
    top = right.astype(BF16)
    rest = right - top.astype(F32)
    middle = rest.astype(BF16)
    low = (rest - middle.astype(F32)).astype(BF16)
    systems = jnp.dot(
        left, jnp.concatenate([top, middle, low], axis=0), preferred_element_type=F32
    )
    sides = [jnp.zeros((8, 128), F32) for _ in range(REACH)]
    for s in range(16):
        for o in range(REACH):
            factor = jnp.broadcast_to(weighted[8 * o : 8 * o + 8, s : s + 1], (8, 128))
            sides[o] = sides[o] + factor * proj_scr[8 * s : 8 * s + 8, :]
    side = jnp.concatenate(sides, axis=0)
    lane32 = lanes((32, 128))
    for r in range(16):
        tile = systems[:, 128 * r : 128 * r + 128]
        if r == 0:
            tile = jnp.where(lane32 >= 96, pltpu.roll(side, 96, 1), tile)
        if r == 1:
            tile = jnp.where(lane32 >= 96, pltpu.roll(side, 64, 1), tile)
        msg[pl.ds(r, 32, stride=16), :] = tile

    home = visits + me_v

    def slot(n):
        return pl.ds(pl.multiple_of(n * 16, 16), 16)

    @pl.loop(0, REACH * visits)
    def send_systems(step):
        o = REACH - 1 - lax.div(step, visits)
        v = lax.rem(me_v + lax.rem(step, visits), visits)

        @pl.when(o * visits + v != home)
        def _():
            pltpu.make_async_remote_copy(
                src_ref=msg.at[slot(o * visits + v), :],
                dst_ref=inbox.at[slot(o * visits + me_v), :],
                send_sem=msg_send,
                recv_sem=msg_sem,
                device_id=(v, lax.rem(me_q + o - 1 + patches, patches)),
                device_id_type=MESH,
            ).start()

    inbox[slot(home), :] = msg[slot(home), :]
    pltpu.make_async_copy(inbox.at[16:], inbox.at[16:], msg_sem).wait()
    total = inbox[0:16, :]
    for n in range(1, REACH * 8):
        total = total + inbox[16 * n : 16 * n + 16, :]

    answer = solve(unpack(total[0:8], total[8:16]))
    answer = jnp.where(lanes((1, 128)) < NB, answer, 0.0)
    coef_row[...] = answer
    coef_box[1, pl.ds(me_v, 1), :] = answer

    @pl.loop(0, REACH * visits)
    def send_coefs(step):
        o = lax.div(step, visits)
        v = lax.rem(me_v + lax.rem(step, visits), visits)

        @pl.when(o * visits + v != home)
        def _():
            pltpu.make_async_remote_copy(
                src_ref=coef_row,
                dst_ref=coef_box.at[o, pl.ds(me_v, 1), :],
                send_sem=coef_send,
                recv_sem=coef_sem,
                device_id=(v, lax.rem(me_q - o + 1 + patches, patches)),
                device_id_type=MESH,
            ).start()

    coef_ref[0] = answer[:, :NB]
    pltpu.make_async_copy(inbox.at[0:31], inbox.at[0:31], coef_sem).wait()

    lane8 = lanes((8, 128))

    def fit(s, held):
        choice = offset_smem[0, s]
        coefs = coef_box[choice]
        model = jnp.dot(
            coefs[:, :SIDE].astype(BF16), image_scr[s], preferred_element_type=F32
        )
        diff = jnp.concatenate(exposures(s), axis=1) - model
        square = diff * diff
        part = square[:, 0:128]
        for t in range(1, 8):
            part = part + square[:, 128 * t : 128 * t + 128]
        return jnp.where(lane8 == s, jnp.sum(part, axis=1, keepdims=True), held)

    held = lax.fori_loop(0, 16, fit, jnp.zeros((8, 128), F32))
    held = held * weights * (1.0 / 1024.0)
    for v in range(8):
        residual_ref[v, 0] = held[v : v + 1, :16]

    pltpu.make_async_copy(sci_recv.at[1:], sci_recv.at[1:], sci_send).wait()
    pltpu.make_async_copy(w_recv.at[1:], w_recv.at[1:], w_send).wait()
    pltpu.make_async_copy(inbox.at[16:], inbox.at[16:], msg_send).wait()
    pltpu.make_async_copy(inbox.at[0:31], inbox.at[0:31], coef_send).wait()


def on_device(template, science, weight, stamp_patch, basis_across, basis_down):
    visits = lax.axis_size("visit")
    patches = lax.axis_size("patch")
    row_table, col_table = tables(basis_across, basis_down)
    stamps = template.reshape(4, 4, SIDE, SIDE).transpose(0, 2, 1, 3).reshape(192, 192)
    weights = jnp.pad(weight.reshape(8, 16).astype(F32), ((0, 0), (0, 112)))
    offset = jnp.mod(stamp_patch.reshape(1, 16) - lax.axis_index("patch") + 1, patches)
    offset_row = jnp.pad(offset, ((0, 0), (0, 112)))
    vmem = pl.BlockSpec(memory_space=pltpu.VMEM)
    dma = pltpu.SemaphoreType.DMA
    return pl.pallas_call(
        functools.partial(kernel, visits, patches),
        out_shape=(
            jax.ShapeDtypeStruct((1, 1, NB), F32),
            jax.ShapeDtypeStruct((8, 1, 1, 16), F32),
        ),
        in_specs=[vmem] * 5
        + [pl.BlockSpec(memory_space=pltpu.SMEM), pl.BlockSpec(memory_space=pl.ANY)],
        out_specs=(vmem, vmem),
        scratch_shapes=[
            pltpu.VMEM((48, SIDE, 512), BF16),
            pltpu.VMEM((STAMP, SIDE, 512), F32),
            pltpu.VMEM((16, SIDE, 1024), BF16),
            pltpu.VMEM((8, 16, 1024), BF16),
            pltpu.VMEM((1024, 128), F32),
            pltpu.VMEM((8, 128), F32),
            pltpu.VMEM((256, 128), F32),
            pltpu.VMEM((128, 128), F32),
            pltpu.VMEM((512, 128), F32),
            pltpu.VMEM((512, 128), F32),
            pltpu.VMEM((1, 128), F32),
            pltpu.VMEM((REACH, 8, 128), F32),
        ]
        + [dma] * 9,
        compiler_params=pltpu.CompilerParams(
            collective_id=0, has_side_effects=True, vmem_limit_bytes=32 * 1024 * 1024
        ),
    )(stamps, row_table, col_table, weights, offset_row, offset, science.reshape(8, 16, 1024))


def solution(mesh):
    return jax.shard_map(
        on_device,
        mesh=mesh,
        in_specs=(
            P("patch", "visit", None, None),
            P("visit", "patch", None, None, None),
            P("visit", "patch", None, None),
            P("patch", "visit", None),
            P(),
            P(),
        ),
        out_specs=(P("visit", "patch", None), P(None, "patch", "visit", None)),
        check_vma=False,
    )
```

time: 637 us -> 64.3 us (0.10)
  waiting for transfers between devices: 541 us -> 0 us
  Pallas kernels: 0 us -> 46.9 us
  local copies, waits for them, and re-layouts: 34.2 us -> 8.77 us
  matrix products: 17.9 us -> 0 us
  starting transfers between devices: 15 us -> 0 us
  between operations: 14.2 us -> 1.05 us
  other arithmetic: 13.7 us -> 7.3 us
    unnamed x4 -> x0, waiting for transfers between devices: 540 us -> none
    pallas_call x0 -> x1, Pallas kernels: none -> 46.9 us  [on_device(): pl.pallas_call(functools.partial(kernel, visits, patches), out_shape=(jax...]
    reshape x8 -> x4, local copies, waits for them, and re-layouts: 26.7 us -> 1.35 us  [the longest x3 1.34 us: on_device(): template.reshape(4, 4, SIDE, SIDE).transpose(0, 2, 1, 3).reshape(192, 192)]
    dot_general x10 -> x0, matrix products: 17.6 us -> none  [the longest x1 6.72 us: basis_images(): jnp.einsum('kyz,szkx->skyx', col_table, across, preferred_element_type=jn...]
    all_to_all x2 -> x0, starting transfers between devices: 14.9 us -> none  [the longest x1 10.1 us: on_device(): lax.all_to_all(weight, 'visit', split_axis=2, concat_axis=0, tiled=True)]
    another operation x5 -> x0, other arithmetic: 8.54 us -> none  [the longest x3 4.6 us: solve_systems(): factor = jnp.linalg.cholesky(matrices)]
    select_n x0 -> x6, other arithmetic: none -> 6.73 us  [the longest x1 4.66 us: tables(): jnp.where((place == tap)[:, None, :], across[None, :, tap, None], row_table)]
  transfers between devices with their start and end apart: 4 -> 0, of which waited for: 3 -> 0; matrix products, arithmetic and copies ran while one was open for 7% -> 0% of each run, Pallas kernels for 0% -> 0%
where the time goes in v1:
time: 64.3 us; the launch traced here: 64 us
  Pallas kernels  46.9 us (73%)
  local copies, waits for them, and re-layouts  8.77 us (14%)
  other arithmetic  7.3 us (11%)
  between operations  1.05 us (2%)
    pallas_call x1, Pallas kernels, on_device(): pl.pallas_call(functools.partial(kernel, visits, patches), out_shape=(jax...  46.9 us
    select_n x1, other arithmetic, tables(): jnp.where((place == tap)[:, None, :], across[None, :, tap, None], row_table)  4.66 us
    unnamed x13, local copies, waits for them, and re-layouts  3.2 us
    broadcast_in_dim x28, local copies, waits for them, and re-layouts, tables(): jnp.where((place == tap)[:, None, :], across[None, :, tap, None], row_table)  2.11 us
    select_n x1, other arithmetic, tables(): col_table = jnp.where(here, grouped[:, None, :, tap, None], col_table)  2.05 us
    broadcast_in_dim x34, local copies, waits for them, and re-layouts, tables(): col_table = jnp.where(here, grouped[:, None, :, tap, None], col_table)  1.79 us
    reshape x3, local copies, waits for them, and re-layouts, on_device(): template.reshape(4, 4, SIDE, SIDE).transpose(0, 2, 1, 3).reshape(192, 192)  1.34 us

profile of v1, /device:TPU:1, one launch (start us, length us, event | category | flops | bytes accessed | tf_op | source)
XLA Modules:
  0.0 64.0 jit_solution(9842381165297582398)
XLA Ops:
  0.6 1.1 %reshape.939 = bf16[4,4,48,48]{3,2,1,0:T(8,128)(2,1)S(1)} reshape(bf16[1,1,16,2304]{3,2,1,0:T(8,128)(2,1)} %param.6) | data formatting | bytes 147456 | tf_op jit(solution)/shard_map/reshape | solution.py:409
  1.8 0.2 reshape.940.stamps_ref
  3.6 0.6 copy-done.1
  4.5 0.1 broadcast_bitcast_fusion.6
  4.8 0.1 broadcast_bitcast_fusion.14
  5.0 4.7 %bitcast_select_fusion.16.row_ref = bf16[48,5632]{1,0:T(8,128)(2,1)S(1)} fusion(pred[6,8,44,128]{3,2,1,0:T(8,128)(4,1)S(1)} %bitcast.229, pred[6,8,44,128]{3,2,1,0:T(8,128)(4,1)S(1)} %bitcast.230, pred[6,8,44,128]{3,2,1,0:T(8,128)(4,1)S(1)} %bitcast.231, pred[6,8,44,128]{3,2,1,0:T(8,128)(4,1)S(1)} %bitcast.232, pred[6,8,44,128]{3,2,1,0:T(8,128)(4,1)S(1)} %bitcast.233, ...), kind=kLoop, calls=%fused_computation.16 | loop fusion | flops 4595712 | bytes 5327872 | tf_op jit(solution)/shard_map/jit(_where)/select_n | solution.py:31
  9.7 0.4 broadcast_and_fusion.16
  10.2 0.7 %copy-done.2 = f32[43,17]{0,1:T(8,128)S(1)} copy-done((f32[43,17]{0,1:T(8,128)S(1)}, f32[43,17]{0,1:T(8,128)}, u32[]{:S(2)}) %copy-start.2) | copy-done | bytes 2948
  10.9 0.1 copy.15
  11.0 0.3 slice_reduce_fusion.16
  11.3 0.1 broadcast_in_dim.890
  11.4 0.1 broadcast_in_dim.884
  11.6 0.1 broadcast_in_dim.878
  11.7 0.1 broadcast_in_dim.872
  11.8 0.1 broadcast_in_dim.866
  11.9 0.1 broadcast_in_dim.860
  12.0 0.1 broadcast_in_dim.854
  12.1 0.1 broadcast_in_dim.848
  12.2 0.1 broadcast_in_dim.842
  12.3 0.1 broadcast_in_dim.836
  12.4 0.1 broadcast_in_dim.830
  12.6 0.1 broadcast_in_dim.824
  12.7 0.1 broadcast_in_dim.818
  12.8 0.1 broadcast_in_dim.812
  12.9 0.1 broadcast_in_dim.806
  13.0 0.1 broadcast_in_dim.800
  13.1 0.1 broadcast_in_dim.794
  13.2 2.0 %bitcast_select_fusion.33.col_ref = bf16[768,256]{1,0:T(8,128)(2,1)S(1)} fusion(pred[16,8,256]{2,1,0:T(8,128)(4,1)S(1)} %get-tuple-element.52, pred[16,8,256]{2,1,0:T(8,128)(4,1)S(1)} %get-tuple-element.51, pred[16,8,256]{2,1,0:T(8,128)(4,1)S(1)} %get-tuple-element.50, pred[16,8,256]{2,1,0:T(8,128)(4,1)S(1)} %get-tuple-element.49, ...), kind=kLoop, calls=%fused_computation.33 | loop fusion | flops 3342336 | bytes 976384 | tf_op jit(solution)/shard_map/jit(_where)/select_n | solution.py:40
  15.3 0.6 %copy-done.4 = s32[1,1,16]{2,1,0:T(1,128)S(1)} copy-done((s32[1,1,16]{2,1,0:T(1,128)S(1)}, s32[1,1,16]{2,1,0:T(1,128)}, u32[]{:S(2)}) %copy-start.4) | copy-done | bytes 88
  16.0 46.9 %shard_map.77 = (f32[1,1,43]{2,1,0:T(1,128)S(1)}, f32[8,1,1,16]{3,2,1,0:T(1,128)S(1)}) custom-call(bf16[192,192]{1,0:T(8,128)(2,1)S(1)} %reshape.940.stamps_ref, bf16[48,5632]{1,0:T(8,128)(2,1)S(1)} %bitcast_select_fusion.16.row_ref, bf16[768,256]{1,0:T(8,128)(2,1)S(1)} %bitcast_select_fusion.33.col_ref, f32[8,128]{1,0:T(8,128)S(1)} %pad_convert_fusion.weight_ref, ...), custom_call_target="tpu_custom_call" | custom-call | tf_op jit(solution)/shard_map/pallas_call | solution.py:415
  62.9 0.5 copy.86
  63.4 0.6 copy.87
  (63 shorter events, 2.3 us)
Async XLA Ops:
  3.5 0.7 %copy-start.1 = (f32[43,17]{0,1:T(8,128)S(1)}, f32[43,17]{0,1:T(8,128)}, u32[]{:S(2)}) copy-start(f32[43,17]{0,1:T(8,128)} %param.10) | copy-start | bytes 8776
  10.2 0.7 %copy-start.2 = (f32[43,17]{0,1:T(8,128)S(1)}, f32[43,17]{0,1:T(8,128)}, u32[]{:S(2)}) copy-start(f32[43,17]{0,1:T(8,128)} %param.11) | copy-start | bytes 8776
  13.2 2.1 %copy-start.3 = (bf16[1,1,8,16]{3,2,1,0:T(8,128)(2,1)S(1)}, bf16[1,1,8,16]{3,2,1,0:T(8,128)(2,1)}, u32[]{:S(2)}) copy-start(bf16[1,1,8,16]{3,2,1,0:T(8,128)(2,1)} %param.8) | copy-start | bytes 772
  13.2 2.8 %copy-start = (bf16[1,1,8,16,1024]{4,3,2,1,0:T(8,128)(2,1)S(1)}, bf16[1,1,8,16,1024]{4,3,2,1,0:T(8,128)(2,1)}, u32[]{:S(2)}) copy-start(bf16[1,1,8,16,1024]{4,3,2,1,0:T(8,128)(2,1)} %param.7) | copy-start | bytes 786436
  15.3 0.7 %copy-start.4 = (s32[1,1,16]{2,1,0:T(1,128)S(1)}, s32[1,1,16]{2,1,0:T(1,128)}, u32[]{:S(2)}) copy-start(s32[1,1,16]{2,1,0:T(1,128)} %param.9) | copy-start | bytes 196

commit v2 on v1

--- a/solution.py
+++ b/solution.py
@@ -20,25 +20,6 @@
 
 def lanes(shape):
     return lax.broadcasted_iota(jnp.int32, shape, len(shape) - 1)
-
-
-def tables(basis_across, basis_down):
-    across = jnp.pad(basis_across.astype(BF16), ((0, 1), (0, 0)))
-    down = jnp.pad(basis_down.astype(BF16), ((0, 5), (0, 0)))
-    place = jnp.arange(SIDE)[:, None] - jnp.arange(128)[None, :] % STAMP
-    row_table = jnp.zeros((SIDE, 44, 128), BF16)
-    for tap in range(TAPS):
-        row_table = jnp.where(
-            (place == tap)[:, None, :], across[None, :, tap, None], row_table
-        )
-    place = jnp.arange(256)[None, :] % 32 - jnp.arange(16)[:, None]
-    same = jnp.arange(8)[:, None] == jnp.arange(256)[None, :] // 32
-    grouped = down.reshape(6, 8, TAPS)
-    col_table = jnp.zeros((6, 16, 8, 256), BF16)
-    for tap in range(TAPS):
-        here = (place == tap)[None, :, None, :] & same[None, None, :, :]
-        col_table = jnp.where(here, grouped[:, None, :, tap, None], col_table)
-    return row_table.reshape(SIDE, 44 * 128), col_table.reshape(6 * 128, 256)
 
 
 def inverse_4x4(m):
@@ -132,15 +113,24 @@
 def kernel(
     visits,
     patches,
-    stamps_ref,
-    row_ref,
-    col_ref,
+    template_ref,
+    across_ref,
+    down_ref,
     weight_ref,
-    offset_ref,
-    offset_smem,
+    patch_ref,
     science_ref,
     coef_ref,
     residual_ref,
+    template_own,
+    across_own,
+    down_own,
+    weight_own,
+    patch_own,
+    across_scr,
+    down_scr,
+    turn_scr,
+    choice_scr,
+    w_own,
     rows_scr,
     wide_scr,
     image_scr,
@@ -154,6 +144,7 @@
     coef_row,
     coef_box,
     own_sem,
+    small_sem,
     sci_send,
     sci_sem,
     w_send,
@@ -173,6 +164,21 @@
         q = lax.rem(me_q + lax.div(step, visits) - 2 + patches, patches)
         return v, q
 
+    small = [
+        pltpu.make_async_copy(source, target, small_sem.at[n])
+        for n, (source, target) in enumerate(
+            (
+                (weight_ref, weight_own),
+                (across_ref, across_own),
+                (down_ref, down_own),
+                (patch_ref, patch_own),
+                (template_ref, template_own),
+            )
+        )
+    ]
+    for copy in small:
+        copy.start()
+
     @pl.loop(0, span * visits)
     def greet(step):
         @pl.when(step != 2 * visits)
@@ -180,17 +186,58 @@
             v, q = peer(step)
             pl.semaphore_signal(barrier, inc=1, device_id=(v, q), device_id_type=MESH)
 
-    own_copy = pltpu.make_async_copy(science_ref.at[me_v], sci_recv.at[me_v], own_sem)
+    own_copy = pltpu.make_async_copy(science_ref.at[0, 0, me_v], sci_recv.at[me_v], own_sem)
     own_copy.start()
-    w_recv[pl.ds(me_v, 1), :] = weight_ref[pl.ds(me_v, 1), :]
-
+    for copy in small:
+        copy.wait()
+    w_own[...] = jnp.concatenate(
+        [weight_own[0, 0].astype(F32), jnp.zeros((8, 112), F32)], axis=1
+    )
+    w_recv[pl.ds(me_v, 1), :] = w_own[pl.ds(me_v, 1), :]
+    tap = lax.broadcasted_iota(jnp.int32, (TAPS, 128), 0)
+    column = lanes((TAPS, 128)) % STAMP
+    backwards = ((column + tap) % STAMP == 0).astype(F32).astype(BF16)
+    forwards = (column == tap).astype(F32).astype(BF16)
+    nothing5 = jnp.zeros((5, 128), F32)
+    across_scr[NB:, :] = nothing5
+    first_axes = (((0,), (0,)), ((), ()))
+    across_scr[0:NB, :] = lax.dot_general(
+        across_own[...].astype(BF16), backwards, first_axes, preferred_element_type=F32
+    )
+    down_scr[NB:, :] = nothing5
+    down_scr[0:NB, :] = lax.dot_general(
+        down_own[...].astype(BF16), forwards, first_axes, preferred_element_type=F32
+    )
+    near = jnp.concatenate([patch_own[0], jnp.zeros((1, 112), jnp.int32)], axis=1)
+    near = lax.rem(near - me_q + 1 + patches, patches).astype(F32)
+    near16 = jnp.broadcast_to(near, (16, 128))
+    diagonal = lanes((16, 128)) == lax.broadcasted_iota(jnp.int32, (16, 128), 0)
+    choice_scr[...] = jnp.broadcast_to(
+        jnp.sum(jnp.where(diagonal, near16, 0.0), axis=1, keepdims=True), (16, 128)
+    )
+    flat = template_own[0, 0].astype(F32)
+    for z in range(SIDE):
+        turn_scr[16 * z : 16 * z + 16, 0:SIDE] = flat[:, SIDE * z : SIDE * z + SIDE]
+    stamps = jnp.concatenate(
+        [
+            jnp.concatenate(
+                [
+                    turn_scr[pl.ds(4 * g + s, SIDE, stride=16), :][:, :SIDE]
+                    for s in range(4)
+                ],
+                axis=1,
+            )
+            for g in range(4)
+        ],
+        axis=0,
+    ).astype(BF16)
     pl.semaphore_wait(barrier, span * visits - 1)
 
     @pl.loop(1, visits)
     def send_science(step):
         v = lax.rem(me_v + step, visits)
         pltpu.make_async_remote_copy(
-            src_ref=weight_ref.at[pl.ds(v, 1), :],
+            src_ref=w_own.at[pl.ds(v, 1), :],
             dst_ref=w_recv.at[pl.ds(me_v, 1), :],
             send_sem=w_send,
             recv_sem=w_sem,
@@ -198,7 +245,7 @@
             device_id_type=MESH,
         ).start()
         pltpu.make_async_remote_copy(
-            src_ref=science_ref.at[v],
+            src_ref=science_ref.at[0, 0, v],
             dst_ref=sci_recv.at[me_v],
             send_sem=sci_send,
             recv_sem=sci_sem,
@@ -206,15 +253,25 @@
             device_id_type=MESH,
         ).start()
 
-    quarter = lax.broadcasted_iota(jnp.int32, (SIDE, 256), 1) % 128 // STAMP
-    masks = [(quarter == s).astype(F32).astype(BF16) for s in range(4)]
-    stamps = stamps_ref[...]
+    shape = (SIDE, 128)
+    past = lax.broadcasted_iota(jnp.int32, shape, 0) - lanes(shape) % STAMP
+    band = (past >= 0) & (past < TAPS)
+    masks = [
+        (band & (lanes(shape) // STAMP == s)).astype(F32).astype(BF16) for s in range(4)
+    ]
     rows_scr[44:48] = jnp.zeros((4, SIDE, 512), BF16)
 
     @pl.loop(0, 22)
     def make_rows(pair):
-        table = row_ref[:, pl.ds(pl.multiple_of(pair * 256, 256), 256)]
-        right = jnp.concatenate([table * m for m in masks], axis=0)
+        right = []
+        for j in range(2):
+            taps = across_scr[pl.ds(2 * pair + j, 1), :]
+            table = pltpu.roll(
+                jnp.broadcast_to(taps, (STAMP, 128)), 0, 1, stride=1, stride_axis=0
+            )
+            table = jnp.concatenate([table, table[: SIDE - STAMP]], axis=0).astype(BF16)
+            right.append(jnp.concatenate([table * m for m in masks], axis=0))
+        right = jnp.concatenate(right, axis=1)
         out = jnp.dot(stamps, right, preferred_element_type=F32).astype(BF16)
         for j in range(2):
             for g in range(4):
@@ -222,10 +279,30 @@
                     SIDE * g : SIDE * g + SIDE, 128 * j : 128 * j + 128
                 ]
 
+    within = lanes((8, 128)) // STAMP - lax.broadcasted_iota(jnp.int32, (8, 128), 0)
+    owner, owner4 = within == 0, within == -4
+
     @pl.loop(0, 6)
     def make_images(group):
         first = pl.multiple_of(group * 8, 8)
-        left = col_ref[pl.ds(pl.multiple_of(group * 128, 128), 128), :]
+        taps = down_scr[pl.ds(first, 8), :]
+        left = jnp.concatenate(
+            [jnp.where(owner, taps, 0.0), jnp.where(owner4, taps, 0.0)], axis=1
+        )
+        left = jnp.concatenate(
+            [left]
+            + [
+                jnp.concatenate(
+                    [
+                        pltpu.roll(left[:, :128], y, 1),
+                        pltpu.roll(left[:, 128:], y, 1),
+                    ],
+                    axis=1,
+                )
+                for y in range(1, 16)
+            ],
+            axis=0,
+        ).astype(BF16)
         for half in range(2):
             right = rows_scr[pl.ds(first, 8), 16 * half : 16 * half + 32, :]
             out = jnp.dot(left, right.reshape(256, 512), preferred_element_type=F32)
@@ -294,9 +371,9 @@
         proj_scr[pl.ds(pl.multiple_of(s * 8, 8), 8), :] = out[48:56]
 
     weights = w_recv[...]
-    offset = jnp.broadcast_to(offset_ref[...], (8, 128))
+    offset = near16[0:8]
     weighted = jnp.concatenate(
-        [jnp.where(offset == o, weights, 0.0) for o in range(REACH)], axis=0
+        [jnp.where(offset == float(o), weights, 0.0) for o in range(REACH)], axis=0
     )
     left = weighted[:, :16].astype(BF16)
     left = jnp.concatenate([left] * 3, axis=1)
@@ -379,8 +456,10 @@
     lane8 = lanes((8, 128))
 
     def fit(s, held):
-        choice = offset_smem[0, s]
-        coefs = coef_box[choice]
+        choice = jnp.broadcast_to(choice_scr[pl.ds(s, 1), :], (8, 128))
+        coefs = coef_box[0]
+        for o in range(1, REACH):
+            coefs = jnp.where(choice == float(o), coef_box[o], coefs)
         model = jnp.dot(
             coefs[:, :SIDE].astype(BF16), image_scr[s], preferred_element_type=F32
         )
@@ -405,11 +484,6 @@
 def on_device(template, science, weight, stamp_patch, basis_across, basis_down):
     visits = lax.axis_size("visit")
     patches = lax.axis_size("patch")
-    row_table, col_table = tables(basis_across, basis_down)
-    stamps = template.reshape(4, 4, SIDE, SIDE).transpose(0, 2, 1, 3).reshape(192, 192)
-    weights = jnp.pad(weight.reshape(8, 16).astype(F32), ((0, 0), (0, 112)))
-    offset = jnp.mod(stamp_patch.reshape(1, 16) - lax.axis_index("patch") + 1, patches)
-    offset_row = jnp.pad(offset, ((0, 0), (0, 112)))
     vmem = pl.BlockSpec(memory_space=pltpu.VMEM)
     dma = pltpu.SemaphoreType.DMA
     return pl.pallas_call(
@@ -418,10 +492,19 @@
             jax.ShapeDtypeStruct((1, 1, NB), F32),
             jax.ShapeDtypeStruct((8, 1, 1, 16), F32),
         ),
-        in_specs=[vmem] * 5
-        + [pl.BlockSpec(memory_space=pltpu.SMEM), pl.BlockSpec(memory_space=pl.ANY)],
+        in_specs=[pl.BlockSpec(memory_space=pltpu.HBM)] * 6,
         out_specs=(vmem, vmem),
         scratch_shapes=[
+            pltpu.VMEM(template.shape, BF16),
+            pltpu.VMEM((TAPS, NB), F32),
+            pltpu.VMEM((TAPS, NB), F32),
+            pltpu.VMEM(weight.shape, BF16),
+            pltpu.VMEM(stamp_patch.shape, jnp.int32),
+            pltpu.VMEM((SIDE, 128), F32),
+            pltpu.VMEM((SIDE, 128), F32),
+            pltpu.VMEM((SIDE * 16, 128), F32),
+            pltpu.VMEM((16, 128), F32),
+            pltpu.VMEM((8, 128), F32),
             pltpu.VMEM((48, SIDE, 512), BF16),
             pltpu.VMEM((STAMP, SIDE, 512), F32),
             pltpu.VMEM((16, SIDE, 1024), BF16),
@@ -435,11 +518,11 @@
             pltpu.VMEM((1, 128), F32),
             pltpu.VMEM((REACH, 8, 128), F32),
         ]
-        + [dma] * 9,
+        + [dma, dma((5,))] + [dma] * 8,
         compiler_params=pltpu.CompilerParams(
-            collective_id=0, has_side_effects=True, vmem_limit_bytes=32 * 1024 * 1024
+            collective_id=0, has_side_effects=True, vmem_limit_bytes=60 * 1024 * 1024
         ),
-    )(stamps, row_table, col_table, weights, offset_row, offset, science.reshape(8, 16, 1024))
+    )(template, basis_across.T, basis_down.T, weight, stamp_patch, science)
 
 
 def solution(mesh):

time: 64.3 us -> 51.3 us (0.80)
  other arithmetic: 7.3 us -> 0 us
  local copies, waits for them, and re-layouts: 8.77 us -> 1.78 us
  Pallas kernels: 46.9 us -> 48.7 us
    select_n x6 -> x0, other arithmetic: 6.73 us -> none  [the longest x1 4.66 us: tables(): jnp.where((place == tap)[:, None, :], across[None, :, tap, None], row_table)]
    broadcast_in_dim x62 -> x0, local copies, waits for them, and re-layouts: 3.9 us -> none  [the longest x28 2.11 us: tables(): jnp.where((place == tap)[:, None, :], across[None, :, tap, None], row_table)]
    pallas_call x1, Pallas kernels: 46.9 us -> 48.7 us  [on_device(): pl.pallas_call(functools.partial(kernel, visits, patches), out_shape=(jax...]
    unnamed x13 -> x4, local copies, waits for them, and re-layouts: 3.2 us -> 1.78 us
    reshape x4 -> x0, local copies, waits for them, and re-layouts: 1.35 us -> none  [the longest x3 1.34 us: on_device(): template.reshape(4, 4, SIDE, SIDE).transpose(0, 2, 1, 3).reshape(192, 192)]
where the time goes in v2:
time: 51.3 us; the launch traced here: 51.2 us
  Pallas kernels  48.7 us (95%)
  local copies, waits for them, and re-layouts  1.78 us (3%)
  between operations  0.65 us (1%)
    pallas_call x1, Pallas kernels, on_device(): pl.pallas_call(functools.partial(kernel, visits, patches), out_shape=(jax...  48.7 us
    unnamed x4, local copies, waits for them, and re-layouts  1.78 us

profile of v2, /device:TPU:1, one launch (start us, length us, event | category | flops | bytes accessed | tf_op | source)
XLA Modules:
  0.0 51.2 jit_solution(1985008829766990213)
XLA Ops:
  0.6 48.7 %shard_map.77 = (f32[1,1,43]{2,1,0:T(1,128)}, f32[8,1,1,16]{3,2,1,0:T(1,128)}) custom-call(bf16[1,1,16,2304]{3,2,1,0:T(8,128)(2,1)} %template_ref.1, f32[17,43]{1,0:T(8,128)} %bitcast.2, f32[17,43]{1,0:T(8,128)} %bitcast.3, bf16[1,1,8,16]{3,2,1,0:T(8,128)(2,1)} %weight_ref.1, s32[1,1,16]{2,1,0:T(1,128)} %patch_ref.1, bf16[1,1,8,16,1024]{4,3,2,1,0:T(8,128)(2,1)} %science_ref.1), custom_call_target="tpu_custom_call" | custom-call | tf_op jit(solution)/shard_map/pallas_call | solution.py:489
  49.4 0.0 copy-start
  49.4 1.2 %copy.10 = f32[1,1,43]{2,1,0:T(1,128)} copy(f32[1,1,43]{2,1,0:T(1,128)} %get-tuple-element.4) | data formatting | bytes 344
  50.6 0.0 copy-done
  50.6 0.6 %copy.11 = f32[8,1,1,16]{3,2,1,0:T(1,128)} copy(f32[8,1,1,16]{3,2,1,0:T(1,128)S(1)} %copy-done) | data formatting | bytes 1024
Async XLA Ops:
  49.4 1.2 %copy-start = (f32[8,1,1,16]{3,2,1,0:T(1,128)S(1)}, f32[8,1,1,16]{3,2,1,0:T(1,128)}, u32[]{:S(2)}) copy-start(f32[8,1,1,16]{3,2,1,0:T(1,128)} %get-tuple-element.5) | copy-start | bytes 1540

commit v3 on v2

--- a/solution.py
+++ b/solution.py
@@ -86,7 +86,7 @@
     return tiles[5][7:8, :]
 
 
-def unpack(low, high):
+def unpack(low, high, right):
     lane = lanes((8, 128))
     row = lax.broadcasted_iota(jnp.int32, (8, 128), 0)
     tiles = [low, high]
@@ -99,11 +99,7 @@
     flipped = square.T[:SIDE]
     full = jnp.where(keep, upper, flipped)
     tiles = [full[8 * t : 8 * t + 8] for t in range(6)]
-    right = jnp.where(
-        lane < 32,
-        jnp.broadcast_to(pltpu.roll(low, 32, 1)[0:1], (8, 128)),
-        jnp.broadcast_to(pltpu.roll(low, 64, 1)[1:2], (8, 128)),
-    )
+    right = jnp.broadcast_to(right, (8, 128))
     right = jnp.where(lane < NB, right, 0.0)
     tiles[5] = jnp.where(row == 7, right, tiles[5])
     tiles[5] = jnp.where((row == 3) & (lane == NB), 1.0, tiles[5])
@@ -138,9 +134,12 @@
     sci_scr,
     w_recv,
     gram_scr,
-    proj_scr,
     msg,
     inbox,
+    side_msg,
+    side_inbox,
+    near_msg,
+    near_inbox,
     coef_row,
     coef_box,
     own_sem,
@@ -151,18 +150,34 @@
     w_sem,
     msg_send,
     msg_sem,
+    side_send,
+    side_sem,
+    near_send,
+    near_sem,
     coef_send,
     coef_sem,
+    row_send,
+    row_sem,
 ):
     me_v = lax.axis_index("visit")
     me_q = lax.axis_index("patch")
     barrier = pltpu.get_barrier_semaphore()
-    span = 2 * REACH - 3
-
-    def peer(step):
-        v = lax.rem(me_v + lax.rem(step, visits), visits)
-        q = lax.rem(me_q + lax.div(step, visits) - 2 + patches, patches)
-        return v, q
+
+    def visit_peer(step):
+        return lax.rem(me_v + step, visits), me_q
+
+    def patch_peer(step):
+        return me_v, lax.rem(me_q + step + patches, patches)
+
+    side_v = lax.rem(me_v, 2)
+    chip = lax.div(me_v, 2)
+    partner = (me_v + 1 - 2 * side_v, me_q)
+
+    def rank(v):
+        return 4 * lax.rem(v, 2) + lax.div(v, 2)
+
+    others = range(1, 8)
+    around = (-2, -1, 1, 2)
 
     small = [
         pltpu.make_async_copy(source, target, small_sem.at[n])
@@ -179,21 +194,17 @@
     for copy in small:
         copy.start()
 
-    @pl.loop(0, span * visits)
-    def greet(step):
-        @pl.when(step != 2 * visits)
-        def _():
-            v, q = peer(step)
-            pl.semaphore_signal(barrier, inc=1, device_id=(v, q), device_id_type=MESH)
-
-    own_copy = pltpu.make_async_copy(science_ref.at[0, 0, me_v], sci_recv.at[me_v], own_sem)
+    for peer in [visit_peer(j) for j in others] + [patch_peer(j) for j in around]:
+        pl.semaphore_signal(barrier, inc=1, device_id=peer, device_id_type=MESH)
+
+    own_copy = pltpu.make_async_copy(science_ref.at[0, 0, me_v], sci_recv.at[rank(me_v)], own_sem)
     own_copy.start()
     for copy in small:
         copy.wait()
     w_own[...] = jnp.concatenate(
         [weight_own[0, 0].astype(F32), jnp.zeros((8, 112), F32)], axis=1
     )
-    w_recv[pl.ds(me_v, 1), :] = w_own[pl.ds(me_v, 1), :]
+    w_recv[pl.ds(rank(me_v), 1), :] = w_own[pl.ds(me_v, 1), :]
     tap = lax.broadcasted_iota(jnp.int32, (TAPS, 128), 0)
     column = lanes((TAPS, 128)) % STAMP
     backwards = ((column + tap) % STAMP == 0).astype(F32).astype(BF16)
@@ -231,27 +242,37 @@
         ],
         axis=0,
     ).astype(BF16)
-    pl.semaphore_wait(barrier, span * visits - 1)
-
-    @pl.loop(1, visits)
-    def send_science(step):
-        v = lax.rem(me_v + step, visits)
+    pl.semaphore_wait(barrier, len(others) + len(around))
+
+    def send(source, target, sems, peer):
         pltpu.make_async_remote_copy(
-            src_ref=w_own.at[pl.ds(v, 1), :],
-            dst_ref=w_recv.at[pl.ds(me_v, 1), :],
-            send_sem=w_send,
-            recv_sem=w_sem,
-            device_id=(v, me_q),
+            src_ref=source,
+            dst_ref=target,
+            send_sem=sems[0],
+            recv_sem=sems[1],
+            device_id=peer,
             device_id_type=MESH,
         ).start()
-        pltpu.make_async_remote_copy(
-            src_ref=science_ref.at[0, 0, v],
-            dst_ref=sci_recv.at[me_v],
-            send_sem=sci_send,
-            recv_sem=sci_sem,
-            device_id=(v, me_q),
-            device_id_type=MESH,
-        ).start()
+
+    def wait(like, sem):
+        pltpu.make_async_copy(like, like, sem).wait()
+
+    for j in (4, 3, 5, 2, 6, 1, 7):
+        peer = visit_peer(j)
+        send(
+            science_ref.at[0, 0, peer[0]],
+            sci_recv.at[rank(me_v)],
+            (sci_send, sci_sem),
+            peer,
+        )
+    for j in (4, 3, 5, 2, 6, 1, 7):
+        peer = visit_peer(j)
+        send(
+            w_own.at[pl.ds(peer[0], 1), :],
+            w_recv.at[pl.ds(rank(me_v), 1), :],
+            (w_send, w_sem),
+            peer,
+        )
 
     shape = (SIDE, 128)
     past = lax.broadcasted_iota(jnp.int32, shape, 0) - lanes(shape) % STAMP
@@ -261,7 +282,7 @@
     ]
     rows_scr[44:48] = jnp.zeros((4, SIDE, 512), BF16)
 
-    @pl.loop(0, 22)
+    @pl.loop(0, 22, unroll=22)
     def make_rows(pair):
         right = []
         for j in range(2):
@@ -282,7 +303,7 @@
     within = lanes((8, 128)) // STAMP - lax.broadcasted_iota(jnp.int32, (8, 128), 0)
     owner, owner4 = within == 0, within == -4
 
-    @pl.loop(0, 6)
+    @pl.loop(0, 6, unroll=6)
     def make_images(group):
         first = pl.multiple_of(group * 8, 8)
         taps = down_scr[pl.ds(first, 8), :]
@@ -312,7 +333,7 @@
     even = lane // STAMP % 2 == 0
     lower = lane < 64
 
-    @pl.loop(0, 8)
+    @pl.loop(0, 8, unroll=8)
     def regroup(quad):
         for g in range(4):
             part = [
@@ -331,33 +352,14 @@
                     s
                 ].astype(BF16)
 
-    own_copy.wait()
-    pltpu.make_async_copy(sci_recv.at[1:], sci_recv.at[1:], sci_sem).wait()
-    pltpu.make_async_copy(w_recv.at[1:], w_recv.at[1:], w_sem).wait()
-
-    for v in range(8):
-        for t in range(8):
-            sci_scr[128 * t + 16 * v : 128 * t + 16 * v + 16, :] = sci_recv[
-                v, :, 128 * t : 128 * t + 128
-            ].astype(F32)
-
-    def exposures(s):
-        return [sci_scr[pl.ds(128 * t + s, 8, stride=16), :] for t in range(8)]
-
-    nothing = jnp.zeros((8, 1024), F32)
     lane16 = lanes((16, 128))
-
-    @pl.loop(0, 16)
+    second_axes = (((1,), (1,)), ((), ()))
+
+    @pl.loop(0, 16, unroll=16)
     def make_grams(s):
         image = image_scr[s]
-        science = jnp.concatenate(exposures(s), axis=1)
-        left = jnp.concatenate(
-            [image, jnp.concatenate([science, nothing], axis=0).astype(BF16)], axis=0
-        )
-        out = lax.dot_general(
-            left, image, (((1,), (1,)), ((), ())), preferred_element_type=F32
-        )
-        out = jnp.concatenate([out, jnp.zeros((64, 80), F32)], axis=1)
+        out = lax.dot_general(image, image, second_axes, preferred_element_type=F32)
+        out = jnp.concatenate([out, jnp.zeros((SIDE, 80), F32)], axis=1)
         packed = jnp.where(
             lane16 < 48,
             out[0:16],
@@ -368,14 +370,12 @@
             ),
         )
         gram_scr[pl.ds(pl.multiple_of(s * 16, 16), 16), :] = packed
-        proj_scr[pl.ds(pl.multiple_of(s * 8, 8), 8), :] = out[48:56]
-
+
+    wait(w_recv.at[1:], w_sem)
     weights = w_recv[...]
     offset = near16[0:8]
-    weighted = jnp.concatenate(
-        [jnp.where(offset == float(o), weights, 0.0) for o in range(REACH)], axis=0
-    )
-    left = weighted[:, :16].astype(BF16)
+    weighted = [jnp.where(offset == float(o), weights, 0.0) for o in range(REACH)]
+    left = jnp.concatenate(weighted, axis=0)[:, :16].astype(BF16)
     left = jnp.concatenate([left] * 3, axis=1)
     right = jnp.concatenate(
         [gram_scr[pl.ds(r, 16, stride=16), :] for r in range(16)], axis=1
@@ -387,79 +387,101 @@
     systems = jnp.dot(
         left, jnp.concatenate([top, middle, low], axis=0), preferred_element_type=F32
     )
-    sides = [jnp.zeros((8, 128), F32) for _ in range(REACH)]
+    for r in range(16):
+        for o in range(REACH):
+            msg[pl.ds(16 * o + r, 8, stride=64), :] = systems[
+                8 * o : 8 * o + 8, 128 * r : 128 * r + 128
+            ]
+
+    def part(n, size):
+        return pl.ds(pl.multiple_of(n * size, size), size)
+
+    send(msg.at[part(1 - side_v, 256), :], inbox, (msg_send, msg_sem), partner)
+
+    own_copy.wait()
+    wait(sci_recv.at[1:], sci_sem)
+    for v in range(8):
+        for t in range(8):
+            sci_scr[128 * t + 16 * v : 128 * t + 16 * v + 16, :] = sci_recv[
+                v, :, 128 * t : 128 * t + 128
+            ].astype(F32)
+
+    def exposures(s):
+        return [sci_scr[pl.ds(128 * t + s, 8, stride=16), :] for t in range(8)]
+
+    sides = [jnp.zeros((8, SIDE), F32) for _ in range(REACH)]
     for s in range(16):
+        science = jnp.concatenate(exposures(s), axis=1).astype(BF16)
+        out = lax.dot_general(
+            science, image_scr[s], second_axes, preferred_element_type=F32
+        )
         for o in range(REACH):
-            factor = jnp.broadcast_to(weighted[8 * o : 8 * o + 8, s : s + 1], (8, 128))
-            sides[o] = sides[o] + factor * proj_scr[8 * s : 8 * s + 8, :]
-    side = jnp.concatenate(sides, axis=0)
-    lane32 = lanes((32, 128))
-    for r in range(16):
-        tile = systems[:, 128 * r : 128 * r + 128]
-        if r == 0:
-            tile = jnp.where(lane32 >= 96, pltpu.roll(side, 96, 1), tile)
-        if r == 1:
-            tile = jnp.where(lane32 >= 96, pltpu.roll(side, 64, 1), tile)
-        msg[pl.ds(r, 32, stride=16), :] = tile
-
-    home = visits + me_v
-
-    def slot(n):
-        return pl.ds(pl.multiple_of(n * 16, 16), 16)
-
-    @pl.loop(0, REACH * visits)
-    def send_systems(step):
-        o = REACH - 1 - lax.div(step, visits)
-        v = lax.rem(me_v + lax.rem(step, visits), visits)
-
-        @pl.when(o * visits + v != home)
-        def _():
-            pltpu.make_async_remote_copy(
-                src_ref=msg.at[slot(o * visits + v), :],
-                dst_ref=inbox.at[slot(o * visits + me_v), :],
-                send_sem=msg_send,
-                recv_sem=msg_sem,
-                device_id=(v, lax.rem(me_q + o - 1 + patches, patches)),
-                device_id_type=MESH,
-            ).start()
-
-    inbox[slot(home), :] = msg[slot(home), :]
-    pltpu.make_async_copy(inbox.at[16:], inbox.at[16:], msg_sem).wait()
-    total = inbox[0:16, :]
-    for n in range(1, REACH * 8):
-        total = total + inbox[16 * n : 16 * n + 16, :]
-
-    answer = solve(unpack(total[0:8], total[8:16]))
+            factor = jnp.broadcast_to(weighted[o][:, s : s + 1], (8, SIDE))
+            sides[o] = sides[o] + factor * out
+    for o in range(REACH):
+        side_msg[pl.ds(o, 8, stride=8), :] = jnp.concatenate(
+            [sides[o], jnp.zeros((8, 80), F32)], axis=1
+        )
+        side_msg[pl.ds(4 + o, 8, stride=8), :] = jnp.zeros((8, 128), F32)
+    send(
+        side_msg.at[part(1 - side_v, 32), :], side_inbox, (side_send, side_sem), partner
+    )
+
+    wait(inbox, msg_sem)
+    summed = msg[part(side_v, 256), :] + inbox[...]
+    for n in range(16):
+        near_msg[n, 0:16, :] = summed[16 * n : 16 * n + 16]
+    wait(side_inbox, side_sem)
+    summed = side_msg[part(side_v, 32), :] + side_inbox[...]
+    for n in range(16):
+        row = 8 * (n // 4) + n % 4
+        near_msg[n, 16:17, :] = summed[row : row + 1]
+    near = [(o, j) for o in range(REACH) for j in range(4) if (o, j) != (1, 0)]
+    near.sort(key=lambda t: -abs(t[0] - 1) - min(t[1], 4 - t[1]))
+    for o, j in near:
+        there = lax.rem(chip + j, 4)
+        send(
+            near_msg.at[4 * there + o],
+            near_inbox.at[4 * o + j],
+            (near_send, near_sem),
+            (2 * there + side_v, patch_peer(o - 1)[1]),
+        )
+    total = near_msg[4 * chip + 1]
+    wait(near_inbox.at[1:], near_sem)
+    for o, j in near:
+        total = total + near_inbox[4 * o + j]
+
+    answer = solve(unpack(total[0:8], total[8:16], total[16:17]))
     answer = jnp.where(lanes((1, 128)) < NB, answer, 0.0)
-    coef_row[...] = answer
-    coef_box[1, pl.ds(me_v, 1), :] = answer
-
-    @pl.loop(0, REACH * visits)
-    def send_coefs(step):
-        o = lax.div(step, visits)
-        v = lax.rem(me_v + lax.rem(step, visits), visits)
-
-        @pl.when(o * visits + v != home)
-        def _():
-            pltpu.make_async_remote_copy(
-                src_ref=coef_row,
-                dst_ref=coef_box.at[o, pl.ds(me_v, 1), :],
-                send_sem=coef_send,
-                recv_sem=coef_sem,
-                device_id=(v, lax.rem(me_q - o + 1 + patches, patches)),
-                device_id_type=MESH,
-            ).start()
-
+    coef_row[pl.ds(side_v, 1), :] = answer
+    mine = pl.ds(side_v, 1)
+    send(coef_row.at[mine, :], coef_row.at[mine, :], (coef_send, coef_sem), partner)
     coef_ref[0] = answer[:, :NB]
-    pltpu.make_async_copy(inbox.at[0:31], inbox.at[0:31], coef_sem).wait()
+    wait(coef_row.at[0:1], coef_sem)
+    for o, j in near:
+        there = lax.rem(chip + j, 4)
+        send(
+            coef_row,
+            coef_box.at[o, chip],
+            (row_send, row_sem),
+            (2 * there + side_v, patch_peer(1 - o)[1]),
+        )
+    coef_box[1, chip] = coef_row[...]
+    wait(inbox.at[0:30], row_sem)
+    coefs_of = [
+        jnp.concatenate(
+            [coef_box[o, x, c : c + 1, :] for c in range(2) for x in range(4)], axis=0
+        )
+        for o in range(REACH)
+    ]
 
     lane8 = lanes((8, 128))
 
     def fit(s, held):
         choice = jnp.broadcast_to(choice_scr[pl.ds(s, 1), :], (8, 128))
-        coefs = coef_box[0]
+        coefs = coefs_of[0]
         for o in range(1, REACH):
-            coefs = jnp.where(choice == float(o), coef_box[o], coefs)
+            coefs = jnp.where(choice == float(o), coefs_of[o], coefs)
         model = jnp.dot(
             coefs[:, :SIDE].astype(BF16), image_scr[s], preferred_element_type=F32
         )
@@ -470,15 +492,19 @@
             part = part + square[:, 128 * t : 128 * t + 128]
         return jnp.where(lane8 == s, jnp.sum(part, axis=1, keepdims=True), held)
 
-    held = lax.fori_loop(0, 16, fit, jnp.zeros((8, 128), F32))
+    held = lax.fori_loop(0, 16, fit, jnp.zeros((8, 128), F32), unroll=16)
     held = held * weights * (1.0 / 1024.0)
     for v in range(8):
-        residual_ref[v, 0] = held[v : v + 1, :16]
-
-    pltpu.make_async_copy(sci_recv.at[1:], sci_recv.at[1:], sci_send).wait()
-    pltpu.make_async_copy(w_recv.at[1:], w_recv.at[1:], w_send).wait()
-    pltpu.make_async_copy(inbox.at[16:], inbox.at[16:], msg_send).wait()
-    pltpu.make_async_copy(inbox.at[0:31], inbox.at[0:31], coef_send).wait()
+        row = 4 * (v % 2) + v // 2
+        residual_ref[v, 0] = held[row : row + 1, :16]
+
+    wait(w_recv.at[1:], w_send)
+    wait(sci_recv.at[1:], sci_send)
+    wait(inbox, msg_send)
+    wait(side_inbox, side_send)
+    wait(near_inbox.at[1:], near_send)
+    wait(coef_row.at[0:1], coef_send)
+    wait(inbox.at[0:30], row_send)
 
 
 def on_device(template, science, weight, stamp_patch, basis_across, basis_down):
@@ -512,13 +538,16 @@
             pltpu.VMEM((1024, 128), F32),
             pltpu.VMEM((8, 128), F32),
             pltpu.VMEM((256, 128), F32),
-            pltpu.VMEM((128, 128), F32),
             pltpu.VMEM((512, 128), F32),
-            pltpu.VMEM((512, 128), F32),
-            pltpu.VMEM((1, 128), F32),
-            pltpu.VMEM((REACH, 8, 128), F32),
+            pltpu.VMEM((256, 128), F32),
+            pltpu.VMEM((64, 128), F32),
+            pltpu.VMEM((32, 128), F32),
+            pltpu.VMEM((16, 17, 128), F32),
+            pltpu.VMEM((16, 17, 128), F32),
+            pltpu.VMEM((2, 128), F32),
+            pltpu.VMEM((REACH, 4, 2, 128), F32),
         ]
-        + [dma, dma((5,))] + [dma] * 8,
+        + [dma, dma((5,))] + [dma] * 14,
         compiler_params=pltpu.CompilerParams(
             collective_id=0, has_side_effects=True, vmem_limit_bytes=60 * 1024 * 1024
         ),

time: 51.3 us -> 39.2 us (0.76)
  Pallas kernels: 48.7 us -> 36.6 us
    pallas_call x1, Pallas kernels: 48.7 us -> 36.6 us  [on_device(): pl.pallas_call(functools.partial(kernel, visits, patches), out_shape=(jax...]
where the time goes in v3:
time: 39.2 us; the launch traced here: 39.1 us
  Pallas kernels  36.6 us (93%)
  local copies, waits for them, and re-layouts  1.78 us (5%)
  between operations  0.65 us (2%)
    pallas_call x1, Pallas kernels, on_device(): pl.pallas_call(functools.partial(kernel, visits, patches), out_shape=(jax...  36.6 us
    unnamed x4, local copies, waits for them, and re-layouts  1.78 us

profile of v3, /device:TPU:1, one launch (start us, length us, event | category | flops | bytes accessed | tf_op | source)
XLA Modules:
  0.0 39.1 jit_solution(10444581770529074529)
XLA Ops:
  0.6 36.6 %shard_map.77 = (f32[1,1,43]{2,1,0:T(1,128)}, f32[8,1,1,16]{3,2,1,0:T(1,128)}) custom-call(bf16[1,1,16,2304]{3,2,1,0:T(8,128)(2,1)} %template_ref.1, f32[17,43]{1,0:T(8,128)} %bitcast.2, f32[17,43]{1,0:T(8,128)} %bitcast.3, bf16[1,1,8,16]{3,2,1,0:T(8,128)(2,1)} %weight_ref.1, s32[1,1,16]{2,1,0:T(1,128)} %patch_ref.1, bf16[1,1,8,16,1024]{4,3,2,1,0:T(8,128)(2,1)} %science_ref.1), custom_call_target="tpu_custom_call" | custom-call | tf_op jit(solution)/shard_map/pallas_call | solution.py:515
  37.3 0.0 copy-start
  37.3 1.2 %copy.10 = f32[1,1,43]{2,1,0:T(1,128)} copy(f32[1,1,43]{2,1,0:T(1,128)} %get-tuple-element.4) | data formatting | bytes 344
  38.5 0.0 copy-done
  38.5 0.6 %copy.11 = f32[8,1,1,16]{3,2,1,0:T(1,128)} copy(f32[8,1,1,16]{3,2,1,0:T(1,128)S(1)} %copy-done) | data formatting | bytes 1024
Async XLA Ops:
  37.3 1.2 %copy-start = (f32[8,1,1,16]{3,2,1,0:T(1,128)S(1)}, f32[8,1,1,16]{3,2,1,0:T(1,128)}, u32[]{:S(2)}) copy-start(f32[8,1,1,16]{3,2,1,0:T(1,128)} %get-tuple-element.5) | copy-start | bytes 1540

commit v4 on v3

--- a/solution.py
+++ b/solution.py
@@ -47,14 +47,15 @@
     )
 
 
-def solve(tiles):
+def invert(tiles):
     lane = lanes((8, 128))
+    row = lax.broadcasted_iota(jnp.int32, (8, 128), 0)
     tiles = list(tiles)
     for block in range(11):
         first = 4 * block
-        tile = tiles[first // 8]
+        home, place = first // 8, first % 8
         rows = [
-            jnp.broadcast_to(tile[(first + c) % 8 : (first + c) % 8 + 1, :], (8, 128))
+            jnp.broadcast_to(tiles[home][place + c : place + c + 1, :], (8, 128))
             for c in range(4)
         ]
         pivot = [[None] * 4 for _ in range(4)]
@@ -73,7 +74,7 @@
             + (inverse[r][2] * rows[2] + inverse[r][3] * rows[3])
             for r in range(4)
         ]
-        for t in range((first + 4) // 8, 6):
+        for t in range(6):
             old = tiles[t]
             cols = [
                 jnp.broadcast_to(old[:, first + c : first + c + 1], (8, 128))
@@ -82,11 +83,15 @@
             change = (cols[0] * scaled[0] + cols[1] * scaled[1]) + (
                 cols[2] * scaled[2] + cols[3] * scaled[3]
             )
-            tiles[t] = jnp.where(inside, 0.0, old) - change
-    return tiles[5][7:8, :]
-
-
-def unpack(low, high, right):
+            new = jnp.where(inside, 0.0, old) - change
+            if t == home:
+                for r in range(4):
+                    new = jnp.where(row == place + r, -scaled[r], new)
+            tiles[t] = new
+    return tiles
+
+
+def unpack(low, high):
     lane = lanes((8, 128))
     row = lax.broadcasted_iota(jnp.int32, (8, 128), 0)
     tiles = [low, high]
@@ -99,9 +104,6 @@
     flipped = square.T[:SIDE]
     full = jnp.where(keep, upper, flipped)
     tiles = [full[8 * t : 8 * t + 8] for t in range(6)]
-    right = jnp.broadcast_to(right, (8, 128))
-    right = jnp.where(lane < NB, right, 0.0)
-    tiles[5] = jnp.where(row == 7, right, tiles[5])
     tiles[5] = jnp.where((row == 3) & (lane == NB), 1.0, tiles[5])
     return tiles
 
@@ -137,7 +139,7 @@
     msg,
     inbox,
     side_msg,
-    side_inbox,
+    side_near,
     near_msg,
     near_inbox,
     coef_row,
@@ -150,12 +152,10 @@
     w_sem,
     msg_send,
     msg_sem,
-    side_send,
-    side_sem,
     near_send,
     near_sem,
-    coef_send,
-    coef_sem,
+    near_side_send,
+    near_side_sem,
     row_send,
     row_sem,
 ):
@@ -178,6 +178,10 @@
 
     others = range(1, 8)
     around = (-2, -1, 1, 2)
+
+    order = (4, 3, 5, 2, 6, 1, 7)
+    for peer in [visit_peer(j) for j in order] + [patch_peer(j) for j in around]:
+        pl.semaphore_signal(barrier, inc=1, device_id=peer, device_id_type=MESH)
 
     small = [
         pltpu.make_async_copy(source, target, small_sem.at[n])
@@ -193,9 +197,6 @@
     ]
     for copy in small:
         copy.start()
-
-    for peer in [visit_peer(j) for j in others] + [patch_peer(j) for j in around]:
-        pl.semaphore_signal(barrier, inc=1, device_id=peer, device_id_type=MESH)
 
     own_copy = pltpu.make_async_copy(science_ref.at[0, 0, me_v], sci_recv.at[rank(me_v)], own_sem)
     own_copy.start()
@@ -257,20 +258,20 @@
     def wait(like, sem):
         pltpu.make_async_copy(like, like, sem).wait()
 
-    for j in (4, 3, 5, 2, 6, 1, 7):
+    for j in order:
+        peer = visit_peer(j)
+        send(
+            w_own.at[pl.ds(peer[0], 1), :],
+            w_recv.at[pl.ds(rank(me_v), 1), :],
+            (w_send, w_sem),
+            peer,
+        )
+    for j in order:
         peer = visit_peer(j)
         send(
             science_ref.at[0, 0, peer[0]],
             sci_recv.at[rank(me_v)],
             (sci_send, sci_sem),
-            peer,
-        )
-    for j in (4, 3, 5, 2, 6, 1, 7):
-        peer = visit_peer(j)
-        send(
-            w_own.at[pl.ds(peer[0], 1), :],
-            w_recv.at[pl.ds(rank(me_v), 1), :],
-            (w_send, w_sem),
             peer,
         )
 
@@ -398,6 +399,21 @@
 
     send(msg.at[part(1 - side_v, 256), :], inbox, (msg_send, msg_sem), partner)
 
+    near = [(o, j) for o in range(REACH) for j in range(4) if (o, j) != (1, 0)]
+    near.sort(key=lambda t: -abs(t[0] - 1) - min(t[1], 4 - t[1]))
+    wait(inbox, msg_sem)
+    summed = msg[part(side_v, 256), :] + inbox[...]
+    for n in range(16):
+        near_msg[n] = summed[16 * n : 16 * n + 16]
+    for o, j in near:
+        there = lax.rem(chip + j, 4)
+        send(
+            near_msg.at[4 * there + o],
+            near_inbox.at[4 * o + j],
+            (near_send, near_sem),
+            (2 * there + side_v, patch_peer(o - 1)[1]),
+        )
+
     own_copy.wait()
     wait(sci_recv.at[1:], sci_sem)
     for v in range(8):
@@ -423,65 +439,54 @@
             [sides[o], jnp.zeros((8, 80), F32)], axis=1
         )
         side_msg[pl.ds(4 + o, 8, stride=8), :] = jnp.zeros((8, 128), F32)
-    send(
-        side_msg.at[part(1 - side_v, 32), :], side_inbox, (side_send, side_sem), partner
-    )
-
-    wait(inbox, msg_sem)
-    summed = msg[part(side_v, 256), :] + inbox[...]
-    for n in range(16):
-        near_msg[n, 0:16, :] = summed[16 * n : 16 * n + 16]
-    wait(side_inbox, side_sem)
-    summed = side_msg[part(side_v, 32), :] + side_inbox[...]
-    for n in range(16):
-        row = 8 * (n // 4) + n % 4
-        near_msg[n, 16:17, :] = summed[row : row + 1]
-    near = [(o, j) for o in range(REACH) for j in range(4) if (o, j) != (1, 0)]
-    near.sort(key=lambda t: -abs(t[0] - 1) - min(t[1], 4 - t[1]))
-    for o, j in near:
-        there = lax.rem(chip + j, 4)
+    every = [(o, j) for o in range(REACH) for j in range(8) if (o, j) != (1, 0)]
+    every.sort(key=lambda t: -abs(t[0] - 1) - (min(t[1], 8 - t[1]) + 1) // 2)
+    for o, j in every:
+        v = visit_peer(j)[0]
         send(
-            near_msg.at[4 * there + o],
-            near_inbox.at[4 * o + j],
-            (near_send, near_sem),
-            (2 * there + side_v, patch_peer(o - 1)[1]),
-        )
+            side_msg.at[pl.ds(8 * rank(v) + o, 1), :],
+            side_near.at[pl.ds(8 * o + j, 1), :],
+            (near_side_send, near_side_sem),
+            (v, patch_peer(o - 1)[1]),
+        )
+
     total = near_msg[4 * chip + 1]
     wait(near_inbox.at[1:], near_sem)
     for o, j in near:
         total = total + near_inbox[4 * o + j]
-
-    answer = solve(unpack(total[0:8], total[8:16], total[16:17]))
+    inverse = invert(unpack(total[0:8], total[8:16]))
+    side_near[8:9, :] = side_msg[pl.ds(8 * rank(me_v) + 1, 1), :]
+    wait(msg.at[0:31, :], near_side_sem)
+    side = jnp.sum(side_near[...], axis=0, keepdims=True)
+    side = jnp.where(lanes((1, 128)) < NB, side, 0.0)
+    side = jnp.broadcast_to(side, (8, 128))
+    across = lanes((8, 128)) - lax.broadcasted_iota(jnp.int32, (8, 128), 0)
+    answer = jnp.zeros((8, 128), F32)
+    for t in range(6):
+        value = jnp.sum(inverse[t] * side, axis=1, keepdims=True)
+        answer = answer + jnp.where(across == 8 * t, value, 0.0)
+    answer = jnp.sum(answer, axis=0, keepdims=True)
     answer = jnp.where(lanes((1, 128)) < NB, answer, 0.0)
-    coef_row[pl.ds(side_v, 1), :] = answer
-    mine = pl.ds(side_v, 1)
-    send(coef_row.at[mine, :], coef_row.at[mine, :], (coef_send, coef_sem), partner)
-    coef_ref[0] = answer[:, :NB]
-    wait(coef_row.at[0:1], coef_sem)
-    for o, j in near:
-        there = lax.rem(chip + j, 4)
+    coef_row[...] = answer
+    place = pl.ds(rank(me_v), 1)
+    for o, j in every:
         send(
             coef_row,
-            coef_box.at[o, chip],
+            coef_box.at[o, place, :],
             (row_send, row_sem),
-            (2 * there + side_v, patch_peer(1 - o)[1]),
-        )
-    coef_box[1, chip] = coef_row[...]
-    wait(inbox.at[0:30], row_sem)
-    coefs_of = [
-        jnp.concatenate(
-            [coef_box[o, x, c : c + 1, :] for c in range(2) for x in range(4)], axis=0
-        )
-        for o in range(REACH)
-    ]
+            (visit_peer(j)[0], patch_peer(1 - o)[1]),
+        )
+    coef_ref[0] = answer[:, :NB]
+    coef_box[1, place, :] = answer
+    wait(msg.at[0:31, :], row_sem)
 
     lane8 = lanes((8, 128))
 
     def fit(s, held):
         choice = jnp.broadcast_to(choice_scr[pl.ds(s, 1), :], (8, 128))
-        coefs = coefs_of[0]
+        coefs = coef_box[0]
         for o in range(1, REACH):
-            coefs = jnp.where(choice == float(o), coefs_of[o], coefs)
+            coefs = jnp.where(choice == float(o), coef_box[o], coefs)
         model = jnp.dot(
             coefs[:, :SIDE].astype(BF16), image_scr[s], preferred_element_type=F32
         )
@@ -501,10 +506,9 @@
     wait(w_recv.at[1:], w_send)
     wait(sci_recv.at[1:], sci_send)
     wait(inbox, msg_send)
-    wait(side_inbox, side_send)
     wait(near_inbox.at[1:], near_send)
-    wait(coef_row.at[0:1], coef_send)
-    wait(inbox.at[0:30], row_send)
+    wait(msg.at[0:31, :], near_side_send)
+    wait(msg.at[0:31, :], row_send)
 
 
 def on_device(template, science, weight, stamp_patch, basis_across, basis_down):
@@ -542,16 +546,21 @@
             pltpu.VMEM((256, 128), F32),
             pltpu.VMEM((64, 128), F32),
             pltpu.VMEM((32, 128), F32),
-            pltpu.VMEM((16, 17, 128), F32),
-            pltpu.VMEM((16, 17, 128), F32),
-            pltpu.VMEM((2, 128), F32),
-            pltpu.VMEM((REACH, 4, 2, 128), F32),
+            pltpu.VMEM((16, 16, 128), F32),
+            pltpu.VMEM((16, 16, 128), F32),
+            pltpu.VMEM((1, 128), F32),
+            pltpu.VMEM((REACH, 8, 128), F32),
         ]
-        + [dma, dma((5,))] + [dma] * 14,
+        + [dma, dma((5,))] + [dma] * 12,
         compiler_params=pltpu.CompilerParams(
-            collective_id=0, has_side_effects=True, vmem_limit_bytes=60 * 1024 * 1024
+            collective_id=0, has_side_effects=True, vmem_limit_bytes=32 * 1024 * 1024
         ),
-    )(template, basis_across.T, basis_down.T, weight, stamp_patch, science)
+    )(
+        *(
+            pltpu.with_memory_space_constraint(x, pltpu.HBM)
+            for x in (template, basis_across.T, basis_down.T, weight, stamp_patch, science)
+        )
+    )
 
 
 def solution(mesh):

time: 39.2 us -> 35.2 us (0.90)
  Pallas kernels: 36.6 us -> 33.3 us
  local copies, waits for them, and re-layouts: 1.78 us -> 1.11 us
    pallas_call x1, Pallas kernels: 36.6 us -> 33.3 us  [on_device(): pl.pallas_call(functools.partial(kernel, visits, patches), out_shape=(jax...]
    unnamed x4 -> x2, local copies, waits for them, and re-layouts: 1.78 us -> 1.11 us
where the time goes in v4:
time: 35.2 us; the launch traced here: 35 us
  Pallas kernels  33.3 us (95%)
  local copies, waits for them, and re-layouts  1.11 us (3%)
  between operations  0.64 us (2%)
    pallas_call x1, Pallas kernels, on_device(): pl.pallas_call(functools.partial(kernel, visits, patches), out_shape=(jax...  33.3 us
    unnamed x2, local copies, waits for them, and re-layouts  1.11 us

profile of v4, /device:TPU:1, one launch (start us, length us, event | category | flops | bytes accessed | tf_op | source)
XLA Modules:
  0.0 35.0 jit_solution(7219427812440173551)
XLA Ops:
  0.6 33.3 %shard_map.77 = (f32[1,1,43]{2,1,0:T(1,128)S(1)}, f32[8,1,1,16]{3,2,1,0:T(1,128)S(1)}) custom-call(bf16[1,1,16,2304]{3,2,1,0:T(8,128)(2,1)} %template_ref.1, f32[17,43]{1,0:T(8,128)} %bitcast.2, f32[17,43]{1,0:T(8,128)} %bitcast.3, bf16[1,1,8,16]{3,2,1,0:T(8,128)(2,1)} %weight_ref.1, s32[1,1,16]{2,1,0:T(1,128)} %patch_ref.1, ...), custom_call_target="tpu_custom_call" | custom-call | tf_op jit(solution)/shard_map/pallas_call | solution.py:519
  33.9 0.5 %copy.10 = f32[1,1,43]{2,1,0:T(1,128)} copy(f32[1,1,43]{2,1,0:T(1,128)S(1)} %get-tuple-element.4) | data formatting | bytes 344
  34.4 0.6 %copy.11 = f32[8,1,1,16]{3,2,1,0:T(1,128)} copy(f32[8,1,1,16]{3,2,1,0:T(1,128)S(1)} %get-tuple-element.5) | data formatting | bytes 1024

commit v5 on v4

--- a/solution.py
+++ b/solution.py
@@ -136,8 +136,7 @@
     sci_scr,
     w_recv,
     gram_scr,
-    msg,
-    inbox,
+    gram_pair,
     side_msg,
     side_near,
     near_msg,
@@ -205,7 +204,8 @@
     w_own[...] = jnp.concatenate(
         [weight_own[0, 0].astype(F32), jnp.zeros((8, 112), F32)], axis=1
     )
-    w_recv[pl.ds(rank(me_v), 1), :] = w_own[pl.ds(me_v, 1), :]
+    for c in range(2):
+        w_recv[pl.ds(2 * rank(me_v) + c, 1), :] = w_own[pl.ds(2 * chip + c, 1), :]
     tap = lax.broadcasted_iota(jnp.int32, (TAPS, 128), 0)
     column = lanes((TAPS, 128)) % STAMP
     backwards = ((column + tap) % STAMP == 0).astype(F32).astype(BF16)
@@ -261,8 +261,8 @@
     for j in order:
         peer = visit_peer(j)
         send(
-            w_own.at[pl.ds(peer[0], 1), :],
-            w_recv.at[pl.ds(rank(me_v), 1), :],
+            w_own.at[pl.ds(2 * lax.div(peer[0], 2), 2), :],
+            w_recv.at[pl.ds(2 * rank(me_v), 2), :],
             (w_send, w_sem),
             peer,
         )
@@ -372,43 +372,51 @@
         )
         gram_scr[pl.ds(pl.multiple_of(s * 16, 16), 16), :] = packed
 
-    wait(w_recv.at[1:], w_sem)
-    weights = w_recv[...]
+    gram_scr[256:264, :] = near16[0:8]
+    send(gram_scr, gram_pair, (msg_send, msg_sem), partner)
+
+    def split(source):
+        full = jnp.concatenate(
+            [source[pl.ds(r, 16, stride=16), :] for r in range(16)], axis=1
+        )
+        top = full.astype(BF16)
+        rest = full - top.astype(F32)
+        middle = rest.astype(BF16)
+        return [top, middle, (rest - middle.astype(F32)).astype(BF16)]
+
+    right = split(gram_scr)
+    wait(gram_pair, msg_sem)
+    right = jnp.concatenate(right + split(gram_pair), axis=0)
+    wait(w_recv.at[2:], w_sem)
+    even_core = lanes((8, 128)) >= 128 * side_v
+    by_core = [w_recv[pl.ds(c, 8, stride=2), :] for c in range(2)]
+    weights = jnp.where(even_core, by_core[0], by_core[1])
     offset = near16[0:8]
     weighted = [jnp.where(offset == float(o), weights, 0.0) for o in range(REACH)]
-    left = jnp.concatenate(weighted, axis=0)[:, :16].astype(BF16)
-    left = jnp.concatenate([left] * 3, axis=1)
-    right = jnp.concatenate(
-        [gram_scr[pl.ds(r, 16, stride=16), :] for r in range(16)], axis=1
-    )
-    top = right.astype(BF16)
-    rest = right - top.astype(F32)
-    middle = rest.astype(BF16)
-    low = (rest - middle.astype(F32)).astype(BF16)
+    theirs = jnp.where(even_core, by_core[1], by_core[0])
+    offset = gram_pair[256:264, :]
+    both = [weighted, [jnp.where(offset == float(o), theirs, 0.0) for o in range(REACH)]]
+    left = []
+    for rows in both:
+        half = jnp.concatenate(
+            [jnp.where(even_core[:4], x[:4], x[4:]) for x in rows], axis=0
+        )
+        left += [half[:, :16].astype(BF16)] * 3
     systems = jnp.dot(
-        left, jnp.concatenate([top, middle, low], axis=0), preferred_element_type=F32
+        jnp.concatenate(left, axis=1), right, preferred_element_type=F32
     )
     for r in range(16):
         for o in range(REACH):
-            msg[pl.ds(16 * o + r, 8, stride=64), :] = systems[
-                8 * o : 8 * o + 8, 128 * r : 128 * r + 128
+            near_msg[pl.ds(16 * o + r, 4, stride=64), :] = systems[
+                4 * o : 4 * o + 4, 128 * r : 128 * r + 128
             ]
-
-    def part(n, size):
-        return pl.ds(pl.multiple_of(n * size, size), size)
-
-    send(msg.at[part(1 - side_v, 256), :], inbox, (msg_send, msg_sem), partner)
 
     near = [(o, j) for o in range(REACH) for j in range(4) if (o, j) != (1, 0)]
     near.sort(key=lambda t: -abs(t[0] - 1) - min(t[1], 4 - t[1]))
-    wait(inbox, msg_sem)
-    summed = msg[part(side_v, 256), :] + inbox[...]
-    for n in range(16):
-        near_msg[n] = summed[16 * n : 16 * n + 16]
     for o, j in near:
         there = lax.rem(chip + j, 4)
         send(
-            near_msg.at[4 * there + o],
+            near_msg.at[pl.ds(pl.multiple_of(64 * there + 16 * o, 16), 16), :],
             near_inbox.at[4 * o + j],
             (near_send, near_sem),
             (2 * there + side_v, patch_peer(o - 1)[1]),
@@ -450,13 +458,13 @@
             (v, patch_peer(o - 1)[1]),
         )
 
-    total = near_msg[4 * chip + 1]
+    total = near_msg[pl.ds(pl.multiple_of(64 * chip + 16, 16), 16), :]
     wait(near_inbox.at[1:], near_sem)
     for o, j in near:
         total = total + near_inbox[4 * o + j]
     inverse = invert(unpack(total[0:8], total[8:16]))
     side_near[8:9, :] = side_msg[pl.ds(8 * rank(me_v) + 1, 1), :]
-    wait(msg.at[0:31, :], near_side_sem)
+    wait(near_msg.at[0:31, :], near_side_sem)
     side = jnp.sum(side_near[...], axis=0, keepdims=True)
     side = jnp.where(lanes((1, 128)) < NB, side, 0.0)
     side = jnp.broadcast_to(side, (8, 128))
@@ -478,7 +486,7 @@
         )
     coef_ref[0] = answer[:, :NB]
     coef_box[1, place, :] = answer
-    wait(msg.at[0:31, :], row_sem)
+    wait(near_msg.at[0:31, :], row_sem)
 
     lane8 = lanes((8, 128))
 
@@ -503,12 +511,12 @@
         row = 4 * (v % 2) + v // 2
         residual_ref[v, 0] = held[row : row + 1, :16]
 
-    wait(w_recv.at[1:], w_send)
+    wait(w_recv.at[2:], w_send)
     wait(sci_recv.at[1:], sci_send)
-    wait(inbox, msg_send)
+    wait(gram_pair, msg_send)
     wait(near_inbox.at[1:], near_send)
-    wait(msg.at[0:31, :], near_side_send)
-    wait(msg.at[0:31, :], row_send)
+    wait(near_msg.at[0:31, :], near_side_send)
+    wait(near_msg.at[0:31, :], row_send)
 
 
 def on_device(template, science, weight, stamp_patch, basis_across, basis_down):
@@ -540,13 +548,12 @@
             pltpu.VMEM((16, SIDE, 1024), BF16),
             pltpu.VMEM((8, 16, 1024), BF16),
             pltpu.VMEM((1024, 128), F32),
-            pltpu.VMEM((8, 128), F32),
-            pltpu.VMEM((256, 128), F32),
-            pltpu.VMEM((512, 128), F32),
-            pltpu.VMEM((256, 128), F32),
+            pltpu.VMEM((16, 128), F32),
+            pltpu.VMEM((264, 128), F32),
+            pltpu.VMEM((264, 128), F32),
             pltpu.VMEM((64, 128), F32),
             pltpu.VMEM((32, 128), F32),
-            pltpu.VMEM((16, 16, 128), F32),
+            pltpu.VMEM((256, 128), F32),
             pltpu.VMEM((16, 16, 128), F32),
             pltpu.VMEM((1, 128), F32),
             pltpu.VMEM((REACH, 8, 128), F32),

time: 35.2 us -> 34.3 us (0.974)
  Pallas kernels: 33.3 us -> 32.3 us
    pallas_call x1, Pallas kernels: 33.3 us -> 32.3 us  [on_device(): pl.pallas_call(functools.partial(kernel, visits, patches), out_shape=(jax...]
where the time goes in v5:
time: 34.3 us; the launch traced here: 34.1 us
  Pallas kernels  32.3 us (94%)
  local copies, waits for them, and re-layouts  1.11 us (3%)
  between operations  0.64 us (2%)
    pallas_call x1, Pallas kernels, on_device(): pl.pallas_call(functools.partial(kernel, visits, patches), out_shape=(jax...  32.3 us
    unnamed x2, local copies, waits for them, and re-layouts  1.11 us

profile of v5, /device:TPU:1, one launch (start us, length us, event | category | flops | bytes accessed | tf_op | source)
XLA Modules:
  0.0 34.1 jit_solution(13913211543802390877)
XLA Ops:
  0.6 32.3 %shard_map.77 = (f32[1,1,43]{2,1,0:T(1,128)S(1)}, f32[8,1,1,16]{3,2,1,0:T(1,128)S(1)}) custom-call(bf16[1,1,16,2304]{3,2,1,0:T(8,128)(2,1)} %template_ref.1, f32[17,43]{1,0:T(8,128)} %bitcast.2, f32[17,43]{1,0:T(8,128)} %bitcast.3, bf16[1,1,8,16]{3,2,1,0:T(8,128)(2,1)} %weight_ref.1, s32[1,1,16]{2,1,0:T(1,128)} %patch_ref.1, ...), custom_call_target="tpu_custom_call" | custom-call | tf_op jit(solution)/shard_map/pallas_call | solution.py:527
  33.0 0.5 %copy.10 = f32[1,1,43]{2,1,0:T(1,128)} copy(f32[1,1,43]{2,1,0:T(1,128)S(1)} %get-tuple-element.4) | data formatting | bytes 344
  33.5 0.6 %copy.11 = f32[8,1,1,16]{3,2,1,0:T(1,128)} copy(f32[8,1,1,16]{3,2,1,0:T(1,128)S(1)} %get-tuple-element.5) | data formatting | bytes 1024

commit v6 on v5

--- a/solution.py
+++ b/solution.py
@@ -243,8 +243,6 @@
         ],
         axis=0,
     ).astype(BF16)
-    pl.semaphore_wait(barrier, len(others) + len(around))
-
     def send(source, target, sems, peer):
         pltpu.make_async_remote_copy(
             src_ref=source,
@@ -257,23 +255,6 @@
 
     def wait(like, sem):
         pltpu.make_async_copy(like, like, sem).wait()
-
-    for j in order:
-        peer = visit_peer(j)
-        send(
-            w_own.at[pl.ds(2 * lax.div(peer[0], 2), 2), :],
-            w_recv.at[pl.ds(2 * rank(me_v), 2), :],
-            (w_send, w_sem),
-            peer,
-        )
-    for j in order:
-        peer = visit_peer(j)
-        send(
-            science_ref.at[0, 0, peer[0]],
-            sci_recv.at[rank(me_v)],
-            (sci_send, sci_sem),
-            peer,
-        )
 
     shape = (SIDE, 128)
     past = lax.broadcasted_iota(jnp.int32, shape, 0) - lanes(shape) % STAMP
@@ -300,6 +281,25 @@
                 rows_scr[2 * pair + j, :, 128 * g : 128 * g + 128] = out[
                     SIDE * g : SIDE * g + SIDE, 128 * j : 128 * j + 128
                 ]
+
+    pl.semaphore_wait(barrier, len(others) + len(around))
+
+    for j in order:
+        peer = visit_peer(j)
+        send(
+            w_own.at[pl.ds(2 * lax.div(peer[0], 2), 2), :],
+            w_recv.at[pl.ds(2 * rank(me_v), 2), :],
+            (w_send, w_sem),
+            peer,
+        )
+    for j in order:
+        peer = visit_peer(j)
+        send(
+            science_ref.at[0, 0, peer[0]],
+            sci_recv.at[rank(me_v)],
+            (sci_send, sci_sem),
+            peer,
+        )
 
     within = lanes((8, 128)) // STAMP - lax.broadcasted_iota(jnp.int32, (8, 128), 0)
     owner, owner4 = within == 0, within == -4
@@ -356,8 +356,7 @@
     lane16 = lanes((16, 128))
     second_axes = (((1,), (1,)), ((), ()))
 
-    @pl.loop(0, 16, unroll=16)
-    def make_grams(s):
+    def make_gram(s):
         image = image_scr[s]
         out = lax.dot_general(image, image, second_axes, preferred_element_type=F32)
         out = jnp.concatenate([out, jnp.zeros((SIDE, 80), F32)], axis=1)
@@ -370,10 +369,14 @@
                 pltpu.roll(out[32:48], 48, 1),
             ),
         )
-        gram_scr[pl.ds(pl.multiple_of(s * 16, 16), 16), :] = packed
+        gram_scr[16 * s : 16 * s + 16, :] = packed
 
     gram_scr[256:264, :] = near16[0:8]
-    send(gram_scr, gram_pair, (msg_send, msg_sem), partner)
+    for first, last in ((0, 6), (6, 11), (11, 16)):
+        for s in range(first, last):
+            make_gram(s)
+        rows = pl.ds(16 * first, 16 * (last - first) + 8 * (last == 16))
+        send(gram_scr.at[rows, :], gram_pair.at[rows, :], (msg_send, msg_sem), partner)
 
     def split(source):
         full = jnp.concatenate(
@@ -519,12 +522,23 @@
     wait(near_msg.at[0:31, :], row_send)
 
 
+def hand_out(coef_ref, residual_ref, coef_out, residual_out, sems):
+    copies = [
+        pltpu.make_async_copy(coef_ref, coef_out, sems.at[0]),
+        pltpu.make_async_copy(residual_ref, residual_out, sems.at[1]),
+    ]
+    for copy in copies:
+        copy.start()
+    for copy in copies:
+        copy.wait()
+
+
 def on_device(template, science, weight, stamp_patch, basis_across, basis_down):
     visits = lax.axis_size("visit")
     patches = lax.axis_size("patch")
     vmem = pl.BlockSpec(memory_space=pltpu.VMEM)
     dma = pltpu.SemaphoreType.DMA
-    return pl.pallas_call(
+    found = pl.pallas_call(
         functools.partial(kernel, visits, patches),
         out_shape=(
             jax.ShapeDtypeStruct((1, 1, NB), F32),
@@ -568,6 +582,16 @@
             for x in (template, basis_across.T, basis_down.T, weight, stamp_patch, science)
         )
     )
+    return pl.pallas_call(
+        hand_out,
+        out_shape=(
+            jax.ShapeDtypeStruct((1, 1, NB), F32),
+            jax.ShapeDtypeStruct((8, 1, 1, 16), F32),
+        ),
+        in_specs=[vmem] * 2,
+        out_specs=[pl.BlockSpec(memory_space=pl.ANY)] * 2,
+        scratch_shapes=[dma((2,))],
+    )(*(pltpu.with_memory_space_constraint(x, pltpu.VMEM) for x in found))
 
 
 def solution(mesh):

time: 34.3 us -> 33.8 us (0.985)
  local copies, waits for them, and re-layouts: 1.11 us -> 0 us
  Pallas kernels: 32.3 us -> 33 us
    unnamed x2 -> x0, local copies, waits for them, and re-layouts: 1.11 us -> none
    pallas_call x0 -> x1, Pallas kernels: none -> 0.62 us  [on_device(): pl.pallas_call(hand_out, out_shape=(jax.ShapeDtypeStruct((1, 1, NB), F32)...]
where the time goes in v6:
time: 33.8 us; the launch traced here: 33.6 us
  Pallas kernels  33 us (98%)
  between operations  0.64 us (2%)
    pallas_call x1, Pallas kernels, on_device(): pl.pallas_call(functools.partial(kernel, visits, patches), out_shape=(jax...  32.3 us

profile of v6, /device:TPU:1, one launch (start us, length us, event | category | flops | bytes accessed | tf_op | source)
XLA Modules:
  0.0 33.6 jit_solution(912606843217908943)
XLA Ops:
  0.6 32.3 %shard_map.77 = (f32[1,1,43]{2,1,0:T(1,128)S(1)}, f32[8,1,1,16]{3,2,1,0:T(1,128)S(1)}) custom-call(bf16[1,1,16,2304]{3,2,1,0:T(8,128)(2,1)} %template_ref.1, f32[17,43]{1,0:T(8,128)} %bitcast.2, f32[17,43]{1,0:T(8,128)} %bitcast.3, bf16[1,1,8,16]{3,2,1,0:T(8,128)(2,1)} %weight_ref.1, s32[1,1,16]{2,1,0:T(1,128)} %patch_ref.1, ...), custom_call_target="tpu_custom_call" | custom-call | tf_op jit(solution)/shard_map/pallas_call | solution.py:541
  33.0 0.6 %shard_map.78 = (f32[1,1,43]{2,1,0:T(1,128)}, f32[8,1,1,16]{3,2,1,0:T(1,128)}) custom-call(f32[1,1,43]{2,1,0:T(1,128)S(1)} %get-tuple-element.4.coef_ref, f32[8,1,1,16]{3,2,1,0:T(1,128)S(1)} %get-tuple-element.5.residual_ref), custom_call_target="tpu_custom_call" | custom-call | tf_op jit(solution)/shard_map/pallas_call | solution.py:585

commit v7 on v6

--- a/solution.py
+++ b/solution.py
@@ -178,55 +178,28 @@
     others = range(1, 8)
     around = (-2, -1, 1, 2)
 
-    order = (4, 3, 5, 2, 6, 1, 7)
-    for peer in [visit_peer(j) for j in order] + [patch_peer(j) for j in around]:
-        pl.semaphore_signal(barrier, inc=1, device_id=peer, device_id_type=MESH)
-
     small = [
         pltpu.make_async_copy(source, target, small_sem.at[n])
         for n, (source, target) in enumerate(
             (
-                (weight_ref, weight_own),
+                (template_ref, template_own),
                 (across_ref, across_own),
                 (down_ref, down_own),
+                (weight_ref, weight_own),
                 (patch_ref, patch_own),
-                (template_ref, template_own),
             )
         )
     ]
     for copy in small:
         copy.start()
 
+    order = (4, 3, 5, 2, 6, 1, 7)
+    for peer in [visit_peer(j) for j in order] + [patch_peer(j) for j in around]:
+        pl.semaphore_signal(barrier, inc=1, device_id=peer, device_id_type=MESH)
+
     own_copy = pltpu.make_async_copy(science_ref.at[0, 0, me_v], sci_recv.at[rank(me_v)], own_sem)
     own_copy.start()
-    for copy in small:
-        copy.wait()
-    w_own[...] = jnp.concatenate(
-        [weight_own[0, 0].astype(F32), jnp.zeros((8, 112), F32)], axis=1
-    )
-    for c in range(2):
-        w_recv[pl.ds(2 * rank(me_v) + c, 1), :] = w_own[pl.ds(2 * chip + c, 1), :]
-    tap = lax.broadcasted_iota(jnp.int32, (TAPS, 128), 0)
-    column = lanes((TAPS, 128)) % STAMP
-    backwards = ((column + tap) % STAMP == 0).astype(F32).astype(BF16)
-    forwards = (column == tap).astype(F32).astype(BF16)
-    nothing5 = jnp.zeros((5, 128), F32)
-    across_scr[NB:, :] = nothing5
-    first_axes = (((0,), (0,)), ((), ()))
-    across_scr[0:NB, :] = lax.dot_general(
-        across_own[...].astype(BF16), backwards, first_axes, preferred_element_type=F32
-    )
-    down_scr[NB:, :] = nothing5
-    down_scr[0:NB, :] = lax.dot_general(
-        down_own[...].astype(BF16), forwards, first_axes, preferred_element_type=F32
-    )
-    near = jnp.concatenate([patch_own[0], jnp.zeros((1, 112), jnp.int32)], axis=1)
-    near = lax.rem(near - me_q + 1 + patches, patches).astype(F32)
-    near16 = jnp.broadcast_to(near, (16, 128))
-    diagonal = lanes((16, 128)) == lax.broadcasted_iota(jnp.int32, (16, 128), 0)
-    choice_scr[...] = jnp.broadcast_to(
-        jnp.sum(jnp.where(diagonal, near16, 0.0), axis=1, keepdims=True), (16, 128)
-    )
+    small[0].wait()
     flat = template_own[0, 0].astype(F32)
     for z in range(SIDE):
         turn_scr[16 * z : 16 * z + 16, 0:SIDE] = flat[:, SIDE * z : SIDE * z + SIDE]
@@ -243,6 +216,34 @@
         ],
         axis=0,
     ).astype(BF16)
+    for copy in small[1:]:
+        copy.wait()
+    w_own[...] = jnp.concatenate(
+        [weight_own[0, 0].astype(F32), jnp.zeros((8, 112), F32)], axis=1
+    )
+    for c in range(2):
+        w_recv[pl.ds(2 * rank(me_v) + c, 1), :] = w_own[pl.ds(2 * chip + c, 1), :]
+    tap = lax.broadcasted_iota(jnp.int32, (TAPS, 128), 0)
+    column = lanes((TAPS, 128)) % STAMP
+    backwards = ((column + tap) % STAMP == 0).astype(F32).astype(BF16)
+    forwards = (column == tap).astype(F32).astype(BF16)
+    nothing5 = jnp.zeros((5, 128), F32)
+    across_scr[NB:, :] = nothing5
+    first_axes = (((0,), (0,)), ((), ()))
+    across_scr[0:NB, :] = lax.dot_general(
+        across_own[...].astype(BF16), backwards, first_axes, preferred_element_type=F32
+    )
+    down_scr[NB:, :] = nothing5
+    down_scr[0:NB, :] = lax.dot_general(
+        down_own[...].astype(BF16), forwards, first_axes, preferred_element_type=F32
+    )
+    near = jnp.concatenate([patch_own[0], jnp.zeros((1, 112), jnp.int32)], axis=1)
+    near = lax.rem(near - me_q + 1 + patches, patches).astype(F32)
+    near16 = jnp.broadcast_to(near, (16, 128))
+    diagonal = lanes((16, 128)) == lax.broadcasted_iota(jnp.int32, (16, 128), 0)
+    choice_scr[...] = jnp.broadcast_to(
+        jnp.sum(jnp.where(diagonal, near16, 0.0), axis=1, keepdims=True), (16, 128)
+    )
     def send(source, target, sems, peer):
         pltpu.make_async_remote_copy(
             src_ref=source,
@@ -463,8 +464,10 @@
 
     total = near_msg[pl.ds(pl.multiple_of(64 * chip + 16, 16), 16), :]
     wait(near_inbox.at[1:], near_sem)
-    for o, j in near:
-        total = total + near_inbox[4 * o + j]
+    terms = [total] + [near_inbox[4 * o + j] for o, j in near]
+    while len(terms) > 1:
+        terms = [a + b for a, b in zip(terms[::2], terms[1::2])]
+    total = terms[0]
     inverse = invert(unpack(total[0:8], total[8:16]))
     side_near[8:9, :] = side_msg[pl.ds(8 * rank(me_v) + 1, 1), :]
     wait(near_msg.at[0:31, :], near_side_sem)

time: 33.8 us -> 33.7 us (level)
  no operation moved by 1% of the time
where the time goes in v7:
time: 33.7 us; the launch traced here: 33.6 us
  Pallas kernels  32.9 us (98%)
  between operations  0.64 us (2%)
    pallas_call x1, Pallas kernels, on_device(): pl.pallas_call(functools.partial(kernel, visits, patches), out_shape=(jax...  32.3 us

profile of v7, /device:TPU:1, one launch (start us, length us, event | category | flops | bytes accessed | tf_op | source)
XLA Modules:
  0.0 33.6 jit_solution(17566085966172543961)
XLA Ops:
  0.6 32.3 %shard_map.77 = (f32[1,1,43]{2,1,0:T(1,128)S(1)}, f32[8,1,1,16]{3,2,1,0:T(1,128)S(1)}) custom-call(bf16[1,1,16,2304]{3,2,1,0:T(8,128)(2,1)} %template_ref.1, f32[17,43]{1,0:T(8,128)} %bitcast.2, f32[17,43]{1,0:T(8,128)} %bitcast.3, bf16[1,1,8,16]{3,2,1,0:T(8,128)(2,1)} %weight_ref.1, s32[1,1,16]{2,1,0:T(1,128)} %patch_ref.1, ...), custom_call_target="tpu_custom_call" | custom-call | tf_op jit(solution)/shard_map/pallas_call | solution.py:544
  33.0 0.6 %shard_map.78 = (f32[1,1,43]{2,1,0:T(1,128)}, f32[8,1,1,16]{3,2,1,0:T(1,128)}) custom-call(f32[1,1,43]{2,1,0:T(1,128)S(1)} %get-tuple-element.4.coef_ref, f32[8,1,1,16]{3,2,1,0:T(1,128)S(1)} %get-tuple-element.5.residual_ref), custom_call_target="tpu_custom_call" | custom-call | tf_op jit(solution)/shard_map/pallas_call | solution.py:588

commit v8 on v7

--- a/solution.py
+++ b/solution.py
@@ -373,7 +373,7 @@
         gram_scr[16 * s : 16 * s + 16, :] = packed
 
     gram_scr[256:264, :] = near16[0:8]
-    for first, last in ((0, 6), (6, 11), (11, 16)):
+    for first, last in ((0, 8), (8, 14), (14, 16)):
         for s in range(first, last):
             make_gram(s)
         rows = pl.ds(16 * first, 16 * (last - first) + 8 * (last == 16))

time: 33.7 us -> 33.7 us (level)
  no operation moved by 1% of the time
where the time goes in v8:
time: 33.7 us; the launch traced here: 33.6 us
  Pallas kernels  32.9 us (98%)
  between operations  0.64 us (2%)
    pallas_call x1, Pallas kernels, on_device(): pl.pallas_call(functools.partial(kernel, visits, patches), out_shape=(jax...  32.3 us

profile of v8, /device:TPU:1, one launch (start us, length us, event | category | flops | bytes accessed | tf_op | source)
XLA Modules:
  0.0 33.6 jit_solution(4061215476536800272)
XLA Ops:
  0.6 32.3 %shard_map.77 = (f32[1,1,43]{2,1,0:T(1,128)S(1)}, f32[8,1,1,16]{3,2,1,0:T(1,128)S(1)}) custom-call(bf16[1,1,16,2304]{3,2,1,0:T(8,128)(2,1)} %template_ref.1, f32[17,43]{1,0:T(8,128)} %bitcast.2, f32[17,43]{1,0:T(8,128)} %bitcast.3, bf16[1,1,8,16]{3,2,1,0:T(8,128)(2,1)} %weight_ref.1, s32[1,1,16]{2,1,0:T(1,128)} %patch_ref.1, ...), custom_call_target="tpu_custom_call" | custom-call | tf_op jit(solution)/shard_map/pallas_call | solution.py:544
  33.0 0.6 %shard_map.78 = (f32[1,1,43]{2,1,0:T(1,128)}, f32[8,1,1,16]{3,2,1,0:T(1,128)}) custom-call(f32[1,1,43]{2,1,0:T(1,128)S(1)} %get-tuple-element.4.coef_ref, f32[8,1,1,16]{3,2,1,0:T(1,128)S(1)} %get-tuple-element.5.residual_ref), custom_call_target="tpu_custom_call" | custom-call | tf_op jit(solution)/shard_map/pallas_call | solution.py:588
